TPU v7x, 256 devices: a whole 4x4x8 slice. The times are simulated.
256 devices in a mesh: dp: 64 (over z, x, core), rep: 4 (over y).
Axes of the slice: x: 4, y: 4, z: 8, core: 2. Of those that a mesh axis runs over, the one named last changes fastest.
Arguments:
- item_tokens: bfloat16 [6144, 24, 256], P(('dp', 'rep')), may hold values from -6 to 6
- owner_index: int32 [6144], P(('dp', 'rep')), may hold values from 0 to 63, as said below
- owner_row: int32 [6144], P(('dp', 'rep')), may hold values from 0 to 15
- parent_tokens: bfloat16 [4096, 32, 256], P(('dp', 'rep')), may hold values from -6 to 6
- cotangent: bfloat16 [4096, 32, 256], P(('dp', 'rep')), may hold values from -30 to 30
- column_gain: bfloat16 [256], replicated, may hold values from 0.5 to 1.5
- column_query: bfloat16 [256, 256], replicated, may hold values from -0.375 to 0.375
- column_key: bfloat16 [256, 256], replicated, may hold values from -0.375 to 0.375
- column_value: bfloat16 [256, 256], replicated, may hold values from -0.375 to 0.375
- column_out: bfloat16 [256, 256], replicated, may hold values from -0.375 to 0.375
- hidden_gain: bfloat16 [256], replicated, may hold values from 0.5 to 1.5
- up_weight: bfloat16 [256, 1024], replicated, may hold values from -0.375 to 0.375
- down_weight: bfloat16 [1024, 256], replicated, may hold values from -0.1875 to 0.1875
- link_weight: bfloat16 [256, 256], replicated, may hold values from -0.375 to 0.375
- parent_gain: bfloat16 [256], replicated, may hold values from 0.5 to 1.5
- parent_query: bfloat16 [256, 256], replicated, may hold values from -0.375 to 0.375
- parent_key: bfloat16 [256, 256], replicated, may hold values from -0.375 to 0.375
- parent_value: bfloat16 [256, 256], replicated, may hold values from -0.375 to 0.375
- parent_out: bfloat16 [256, 256], replicated, may hold values from -0.375 to 0.375
Outputs:
- parent_states: bfloat16 [4096, 32, 256], P(('dp', 'rep'))
- grad_column_gain: float32 [256], replicated
- grad_column_query: float32 [256, 256], replicated
- grad_column_key: float32 [256, 256], replicated
- grad_column_value: float32 [256, 256], replicated
- grad_column_out: float32 [256, 256], replicated
- grad_hidden_gain: float32 [256], replicated
- grad_up_weight: float32 [256, 1024], replicated
- grad_down_weight: float32 [1024, 256], replicated
- grad_link_weight: float32 [256, 256], replicated
- grad_parent_gain: float32 [256], replicated
- grad_parent_query: float32 [256, 256], replicated
- grad_parent_key: float32 [256, 256], replicated
- grad_parent_value: float32 [256, 256], replicated
- grad_parent_out: float32 [256, 256], replicated
Inputs may be any that keep to these rules, and one draw needn't show every extreme that they name: `owner_index`: among the 24 transactions of one device no owner is named more than 2 times; in each group of devices along dp that share an index along rep, one owner is named exactly 2 times by every device.
All inputs are finite; a program needn't handle non-finite values.
Results may differ from a plain program's by a relative error of at most 0.03.
Values may be sent and summed in bfloat16 or wider, within the bound.
A program may use at most 64 MiB of HBM per device.

v0:
```python
import math

import jax
import jax.numpy as jnp
from jax import lax
from jax.sharding import PartitionSpec as P

HEADS = 8


EPSILON = 1e-06


def scaled_norm(values, gain_vec):
    mean_square = jnp.mean(values * values, axis=-1, keepdims=True)
    return values * lax.rsqrt(mean_square + EPSILON) * gain_vec


def project(inputs, matrix):
    return jnp.einsum("...i,ij->...j", inputs.astype(jnp.float32), matrix)


def attention(tokens, gain_vec, query_matrix, key_matrix, value_matrix, out_matrix, head_count):
    row_count, length, feature = tokens.shape
    head_dim = feature // head_count
    normed = scaled_norm(tokens.astype(jnp.float32), gain_vec).astype(jnp.bfloat16)
    queries = (
        project(normed, query_matrix)
        .astype(jnp.bfloat16)
        .reshape(row_count, length, head_count, head_dim)
    )
    key_rows = (
        project(normed, key_matrix)
        .astype(jnp.bfloat16)
        .reshape(row_count, length, head_count, head_dim)
    )
    value_rows = (
        project(normed, value_matrix)
        .astype(jnp.bfloat16)
        .reshape(row_count, length, head_count, head_dim)
    )
    scores = jnp.einsum(
        "blhd,bmhd->bhlm", queries, key_rows, preferred_element_type=jnp.float32
    ) * head_dim ** (-0.5)
    weights = jax.nn.softmax(scores, axis=-1).astype(jnp.bfloat16)
    mixture = jnp.einsum("bhlm,bmhd->blhd", weights, value_rows, preferred_element_type=jnp.float32)
    mixture = mixture.reshape(row_count, length, feature).astype(jnp.bfloat16)
    return project(mixture, out_matrix)


def encode_rows(tokens, params):
    (
        gain_first,
        query_matrix,
        key_matrix,
        value_matrix,
        out_matrix,
        gain_second,
        up_matrix,
        down_matrix,
    ) = params
    stream = (
        tokens.astype(jnp.float32)
        + attention(tokens, gain_first, query_matrix, key_matrix, value_matrix, out_matrix, HEADS)
    ).astype(jnp.bfloat16)
    normed = scaled_norm(stream.astype(jnp.float32), gain_second).astype(jnp.bfloat16)
    hidden = jax.nn.gelu(project(normed, up_matrix), approximate=True).astype(jnp.bfloat16)
    output_rows = stream.astype(jnp.float32) + project(hidden, down_matrix)
    return jnp.mean(output_rows, axis=1).astype(jnp.bfloat16)


def parent_forward(tokens, pooled, params):
    link_matrix, gain_vec, query_matrix, key_matrix, value_matrix, out_matrix = params
    linked = project(pooled, link_matrix)
    based = (tokens.astype(jnp.float32) + linked[:, None, :]).astype(jnp.bfloat16)
    return based.astype(jnp.float32) + attention(
        based, gain_vec, query_matrix, key_matrix, value_matrix, out_matrix, HEADS
    )


def body(
    item_tokens,
    owner_index,
    owner_row,
    parent_tokens,
    cotangent,
    column_gain,
    column_query,
    column_key,
    column_value,
    column_out,
    hidden_gain,
    up_weight,
    down_weight,
    link_weight,
    parent_gain,
    parent_query,
    parent_key,
    parent_value,
    parent_out,
):
    item_params = tuple(
        (
            weight.astype(jnp.float32)
            for weight in (
                column_gain,
                column_query,
                column_key,
                column_value,
                column_out,
                hidden_gain,
                up_weight,
                down_weight,
            )
        )
    )
    parent_params = tuple(
        (
            weight.astype(jnp.float32)
            for weight in (
                link_weight,
                parent_gain,
                parent_query,
                parent_key,
                parent_value,
                parent_out,
            )
        )
    )
    dp_count = lax.axis_size("dp")
    rep_count = lax.axis_size("rep")
    item_count = item_tokens.shape[0]
    parent_count = parent_tokens.shape[0]
    feature = item_tokens.shape[2]
    embedded, item_pullback = jax.vjp(lambda params: encode_rows(item_tokens, params), item_params)
    slot_count = max(2, 2 * item_count // dp_count)
    positions = jnp.arange(item_count)
    earlier = (owner_index[None, :] == owner_index[:, None]) & (
        positions[None, :] < positions[:, None]
    )
    slot_index = owner_index * slot_count + jnp.sum(earlier.astype(jnp.int32), axis=1)
    placing = slot_index[None, :] == jnp.arange(dp_count * slot_count)[:, None]
    send_rows = jnp.dot(
        placing.astype(jnp.bfloat16), embedded, preferred_element_type=jnp.float32
    ).astype(jnp.bfloat16)
    send_ids = jnp.sum(placing.astype(jnp.int32) * (owner_row + 1)[None, :], axis=1)
    got_rows, got_ids = (
        lax.all_to_all(
            send_rows.reshape(dp_count, slot_count, feature),
            "dp",
            split_axis=0,
            concat_axis=0,
            tiled=True,
        ),
        lax.all_to_all(
            send_ids.reshape(dp_count, slot_count), "dp", split_axis=0, concat_axis=0, tiled=True
        ),
    )
    got_rows = got_rows.reshape(dp_count * slot_count, feature)
    member = got_ids.reshape(-1)[None, :] == jnp.arange(1, parent_count + 1)[:, None]
    counts = jnp.sum(member.astype(jnp.float32), axis=1)
    sum_rows = jnp.dot(member.astype(jnp.bfloat16), got_rows, preferred_element_type=jnp.float32)
    divisor = jnp.maximum(counts, 1.0)[:, None]
    pooled = (sum_rows / divisor).astype(jnp.bfloat16)
    states, parent_pullback = jax.vjp(
        lambda params, pooled_in: parent_forward(parent_tokens, pooled_in, params),
        parent_params,
        pooled,
    )
    loss_scale = 1.0 / math.sqrt(parent_count * dp_count * rep_count * parent_tokens.shape[1])
    parent_grads, pooled_grad = parent_pullback(cotangent.astype(jnp.float32) * loss_scale)
    sum_grad = pooled_grad.astype(jnp.float32) / divisor
    slot_grad = jnp.dot(member.T.astype(jnp.float32), sum_grad).astype(jnp.bfloat16)
    returned = lax.all_to_all(
        slot_grad.reshape(dp_count, slot_count, feature),
        "dp",
        split_axis=0,
        concat_axis=0,
        tiled=True,
    )
    item_grad = jnp.dot(
        placing.T.astype(jnp.bfloat16),
        returned.reshape(dp_count * slot_count, feature),
        preferred_element_type=jnp.float32,
    ).astype(jnp.bfloat16)
    item_grads = item_pullback(item_grad)[0]
    gradients = tuple(item_grads) + tuple(parent_grads)
    flattened = jnp.concatenate([gradient.reshape(dp_count, -1) for gradient in gradients], axis=1)
    summed = lax.psum(flattened, ("dp", "rep"))
    outputs = []
    offset = 0
    for gradient in gradients:
        extent = gradient.size // dp_count
        outputs.append(summed[:, offset : offset + extent].reshape(gradient.shape))
        offset = offset + extent
    return (states.astype(jnp.bfloat16),) + tuple(outputs)


def solution(mesh):
    return jax.shard_map(
        body,
        mesh=mesh,
        in_specs=(
            P(("dp", "rep"), None, None),
            P(("dp", "rep")),
            P(("dp", "rep")),
            P(("dp", "rep"), None, None),
            P(("dp", "rep"), None, None),
            P(),
            P(),
            P(),
            P(),
            P(),
            P(),
            P(),
            P(),
            P(),
            P(),
            P(),
            P(),
            P(),
            P(),
        ),
        out_specs=(
            P(("dp", "rep"), None, None),
            P(),
            P(),
            P(),
            P(),
            P(),
            P(),
            P(),
            P(),
            P(),
            P(),
            P(),
            P(),
            P(),
            P(),
        ),
        check_vma=False,
    )
```

profile of v0, /device:TPU:2, one launch (start us, length us, event | category | flops | bytes accessed | tf_op | source)
XLA Modules:
  0.0 495.1 jit_solution(10085192183573673747)
XLA Ops:
  9.6 12.2 %all-to-all-start = ((s32[64,1,2]{2,1,0:T(1,128)}), s32[64,1,2]{2,1,0:T(1,128)}, u32[]{:S(2)}, u32[]{:S(2)}) async-start(s32[64,1,2]{2,1,0:T(1,128)} %bitcast), calls=%async_computation | async-start | bytes 65536 | tf_op jit(solution)/shard_map/all_to_all | solution.py:155
  33.1 6.5 %fusion.158 = (f32[24,8,24]{2,1,0:T(8,128)S(1)}, f32[24,8,24,24]{2,3,1,0:T(8,128)S(1)}) fusion(f32[24,8,24,24]{2,3,1,0:T(8,128)S(1)} %fusion.58), kind=kOutput, calls=%fused_computation.219 | output fusion | flops 442391 | bytes 903168 | tf_op jit(solution)/shard_map/jvp()/sub | solution.py:45
  42.4 2.7 convert_element_type.273
  51.6 2.3 copy.155
  54.6 11.0 %all-to-all-start.1 = ((bf16[64,2,256]{2,1,0:T(2,128)(2,1)}), bf16[64,2,256]{2,1,0:T(2,128)(2,1)S(1)}, u32[]{:S(2)}, u32[]{:S(2)}) async-start(bf16[64,2,256]{2,1,0:T(2,128)(2,1)} %reshape.275), calls=%async_computation.1 | async-start | bytes 131072 | tf_op jit(solution)/shard_map/all_to_all | solution.py:148
  66.2 2.1 reduce.3
  69.4 5.1 %all-to-all-done.1 = bf16[64,2,256]{2,1,0:T(2,128)(2,1)S(1)} async-done(((bf16[64,2,256]{2,1,0:T(2,128)(2,1)}), bf16[64,2,256]{2,1,0:T(2,128)(2,1)S(1)}, u32[]{:S(2)}, u32[]{:S(2)}) %all-to-all-start.1) | async-done | bytes 65568 | tf_op jit(solution)/shard_map/all_to_all | solution.py:148
  79.1 2.0 convolution_convert_fusion.23
  81.1 2.0 convolution_convert_fusion.24
  84.0 2.4 reshape.277
  86.5 2.4 reshape.278
  88.9 2.4 reshape.279
  91.3 4.5 fusion.159
  96.7 3.7 convolution_convert_fusion.9
  107.5 2.6 reshape.283
  110.1 2.2 convolution_bitcast_fusion.3
  117.2 2.6 reshape.282
  121.5 2.1 convolution_bitcast_fusion.2
  125.4 2.4 convolution_bitcast_fusion.9
  129.5 2.4 fusion.79
  133.6 2.1 fusion.76
  138.3 5.6 %all-to-all-start.2 = ((bf16[64,2,256]{2,1,0:T(2,128)(2,1)}), bf16[64,2,256]{2,1,0:T(2,128)(2,1)S(1)}, u32[]{:S(2)}, u32[]{:S(2)}) async-start(bf16[64,2,256]{2,1,0:T(2,128)(2,1)} %reshape.284), calls=%async_computation.2 | async-start | bytes 131072 | tf_op jit(solution)/shard_map/all_to_all | solution.py:174
  147.5 5.4 %all-to-all-done.2 = bf16[64,2,256]{2,1,0:T(2,128)(2,1)S(1)} async-done(((bf16[64,2,256]{2,1,0:T(2,128)(2,1)}), bf16[64,2,256]{2,1,0:T(2,128)(2,1)S(1)}, u32[]{:S(2)}, u32[]{:S(2)}) %all-to-all-start.2) | async-done | bytes 65568 | tf_op jit(solution)/shard_map/all_to_all | solution.py:174
  154.6 3.8 convolution_bitcast_fusion
  165.7 2.8 fusion.10
  169.9 2.1 fusion.25
  179.6 2.9 reshape.296
  187.2 2.2 convolution_bitcast_fusion.5
  194.5 6.4 %concatenate.3 = f32[64,17420]{1,0:T(8,128)} concatenate(f32[64,4]{1,0:T(8,128)S(1)} %reshape.290, f32[64,1024]{1,0:T(8,128)} %reshape.291, f32[64,1024]{1,0:T(8,128)} %reshape.292, f32[64,1024]{1,0:T(8,128)} %reshape.293, f32[64,1024]{1,0:T(8,128)} %reshape.294, f32[64,4]{1,0:T(8,128)S(1)} %reshape.295, f32[64,4096]{1,0:T(8,128)S(1)} %copy-done.8, f32[64,4096]{1,0:T(8,128)S(1)} %reshape.297, ...), dimensions={1} | concatenate | bytes 8919040 | tf_op jit(solution)/shard_map/concatenate | solution.py:188
  203.3 265.1 %all-reduce.2.cloned.1.call-done = f32[64,17420]{1,0:T(8,128)} async-done(((f32[64,17420]{1,0:T(8,128)}), f32[64,17420]{1,0:T(8,128)}) %all-reduce.2.cloned.1.call-update) | async-done | bytes 4459536 | tf_op jit(solution)/shard_map/psum | solution.py:189
  471.3 3.2 fusion.155
  475.3 2.2 fusion.157
  (250 shorter events, 100.5 us)
Async XLA Ops:
  7.2 40.7 %copy-start = (bf16[256,1024]{1,0:T(8,128)(2,1)S(1)}, bf16[256,1024]{1,0:T(8,128)(2,1)}, u32[]{:S(2)}) copy-start(bf16[256,1024]{1,0:T(8,128)(2,1)} %param.30) | copy-start | bytes 1572868
  8.8 40.7 %copy-start.61 = (s32[24]{0:T(128)}, s32[24]{0:T(128)S(1)}, u32[]{:S(2)}) copy-start(s32[24]{0:T(128)S(1)} %get-tuple-element.46) | copy-start | bytes 292
  9.6 45.0 %all-to-all-start = ((s32[64,1,2]{2,1,0:T(1,128)}), s32[64,1,2]{2,1,0:T(1,128)}, u32[]{:S(2)}, u32[]{:S(2)}) async-start(s32[64,1,2]{2,1,0:T(1,128)} %bitcast), calls=%async_computation | async-start | bytes 65536 | tf_op jit(solution)/shard_map/all_to_all | solution.py:155
  22.5 7.2 %copy-start.69 = (f32[256]{0:T(256)}, f32[256]{0:T(256)S(1)}, u32[]{:S(2)}) copy-start(f32[256]{0:T(256)S(1)} %convert_element_type.265) | copy-start | bytes 3076
  23.2 24.1 %copy-start.56 = (f32[256]{0:T(256)}, f32[256]{0:T(256)S(1)}, u32[]{:S(2)}) copy-start(f32[256]{0:T(256)S(1)} %convert_element_type.276) | copy-start | bytes 3076
  24.3 5.4 %copy-start.54 = (f32[24,24]{1,0:T(8,128)}, f32[24,24]{1,0:T(8,128)S(1)}, u32[]{:S(2)}) copy-start(f32[24,24]{1,0:T(8,128)S(1)} %add_rsqrt_fusion) | copy-start | bytes 6916
  33.1 7.2 %copy-start.6 = (bf16[24,24,8,32]{3,2,1,0:T(8,128)(2,1)S(1)}, bf16[24,24,8,32]{3,2,1,0:T(8,128)(2,1)}, u32[]{:S(2)}) copy-start(bf16[24,24,8,32]{3,2,1,0:T(8,128)(2,1)} %reshape.272) | copy-start | bytes 884740
  51.1 24.1 %copy-start.63 = (s32[16]{0:T(128)}, s32[16]{0:T(128)S(1)}, u32[]{:S(2)}) copy-start(s32[16]{0:T(128)S(1)} %iota_add_fusion) | copy-start | bytes 196
  54.6 19.9 %all-to-all-start.1 = ((bf16[64,2,256]{2,1,0:T(2,128)(2,1)}), bf16[64,2,256]{2,1,0:T(2,128)(2,1)S(1)}, u32[]{:S(2)}, u32[]{:S(2)}) async-start(bf16[64,2,256]{2,1,0:T(2,128)(2,1)} %reshape.275), calls=%async_computation.1 | async-start | bytes 131072 | tf_op jit(solution)/shard_map/all_to_all | solution.py:148
  69.2 6.0 %copy-start.60 = (s32[128]{0:T(128)}, s32[128]{0:T(128)S(1)}, u32[]{:S(2)}) copy-start(s32[128]{0:T(128)S(1)} %eq.47) | copy-start | bytes 1540
  69.4 5.8 %copy-start.64 = (f32[16]{0:T(128)}, f32[16]{0:T(128)S(1)}, u32[]{:S(2)}) copy-start(f32[16]{0:T(128)S(1)} %broadcast_maximum_fusion) | copy-start | bytes 196
  75.2 7.9 %copy-start.11 = (bf16[16,32,256]{2,1,0:T(8,128)(2,1)S(1)}, bf16[16,32,256]{2,1,0:T(8,128)(2,1)}, u32[]{:S(2)}) copy-start(bf16[16,32,256]{2,1,0:T(8,128)(2,1)} %param.22) | copy-start | bytes 786436
  75.2 7.9 %copy-start.42 = (bf16[256,256]{1,0:T(8,128)(2,1)S(1)}, bf16[256,256]{1,0:T(8,128)(2,1)}, u32[]{:S(2)}) copy-start(bf16[256,256]{1,0:T(8,128)(2,1)} %param.36) | copy-start | bytes 393220
  75.2 7.9 %copy-start.58 = (f32[256]{0:T(256)S(1)}, f32[256]{0:T(256)}, u32[]{:S(2)}) copy-start(f32[256]{0:T(256)} %convert_element_type.285) | copy-start | bytes 3076
  79.0 9.8 %copy-start.48 = (f32[16,32]{1,0:T(8,128)}, f32[16,32]{1,0:T(8,128)S(1)}, u32[]{:S(2)}) copy-start(f32[16,32]{1,0:T(8,128)S(1)} %fusion.78) | copy-start | bytes 6148
  79.1 9.8 %copy-start.51 = (f32[16,32]{1,0:T(8,128)}, f32[16,32]{1,0:T(8,128)S(1)}, u32[]{:S(2)}) copy-start(f32[16,32]{1,0:T(8,128)S(1)} %fusion.115) | copy-start | bytes 6148
  106.0 4.0 copy-start.52
  106.0 4.0 copy-start.59
  110.1 4.5 copy-start.43
  125.4 6.5 %copy-start.49 = (f32[16,32]{1,0:T(8,128)S(1)}, f32[16,32]{1,0:T(8,128)}, u32[]{:S(2)}) copy-start(f32[16,32]{1,0:T(8,128)} %copy-done.48) | copy-start | bytes 6148
  138.3 14.6 %all-to-all-start.2 = ((bf16[64,2,256]{2,1,0:T(2,128)(2,1)}), bf16[64,2,256]{2,1,0:T(2,128)(2,1)S(1)}, u32[]{:S(2)}, u32[]{:S(2)}) async-start(bf16[64,2,256]{2,1,0:T(2,128)(2,1)} %reshape.284), calls=%async_computation.2 | async-start | bytes 131072 | tf_op jit(solution)/shard_map/all_to_all | solution.py:174
  143.9 324.6 %all-reduce.2.cloned.1.call-start = ((), (), s32[]{:S(2)}) async-start(), calls=%async_computation.3 | async-start | bytes 8978432 | tf_op jit(solution)/shard_map/psum | solution.py:189
  154.6 3.8 copy-start.66
  179.4 3.8 copy-start.62
  186.4 6.4 %copy-start.67 = (bf16[256,256]{1,0:T(8,128)(2,1)S(1)}, bf16[256,256]{1,0:T(8,128)(2,1)}, u32[]{:S(2)}) copy-start(bf16[256,256]{1,0:T(8,128)(2,1)} %param.27) | copy-start | bytes 393220
  187.1 7.3 %copy-start.8 = (f32[64,4096]{1,0:T(8,128)S(1)}, f32[64,4096]{1,0:T(8,128)}, u32[]{:S(2)}) copy-start(f32[64,4096]{1,0:T(8,128)} %reshape.296) | copy-start | bytes 3145732
  187.1 7.3 %copy-start.22 = (f32[64,1024]{1,0:T(8,128)S(1)}, f32[64,1024]{1,0:T(8,128)}, u32[]{:S(2)}) copy-start(f32[64,1024]{1,0:T(8,128)} %reshape.300) | copy-start | bytes 786436
  187.2 7.3 %copy-start.23 = (f32[64,1024]{1,0:T(8,128)S(1)}, f32[64,1024]{1,0:T(8,128)}, u32[]{:S(2)}) copy-start(f32[64,1024]{1,0:T(8,128)} %reshape.301) | copy-start | bytes 786436
  187.2 7.3 %copy-start.24 = (f32[64,1024]{1,0:T(8,128)S(1)}, f32[64,1024]{1,0:T(8,128)}, u32[]{:S(2)}) copy-start(f32[64,1024]{1,0:T(8,128)} %reshape.303) | copy-start | bytes 786436
  187.2 7.3 %copy-start.38 = (f32[64,4]{1,0:T(8,128)S(1)}, f32[64,4]{1,0:T(8,128)}, u32[]{:S(2)}) copy-start(f32[64,4]{1,0:T(8,128)} %reshape.299) | copy-start | bytes 3076
  478.6 5.1 %copy-start.25 = (f32[64,1024]{1,0:T(8,128)S(1)}, f32[64,1024]{1,0:T(8,128)}, u32[]{:S(2)}) copy-start(f32[64,1024]{1,0:T(8,128)} %get-tuple-element.24) | copy-start | bytes 786436
  483.7 4.4 copy-start.1
  (43 other events, 82.2 us)
Sparse Core Ops, SparseCore 0:
  201.1 267.3 all-reduce.1
where the time goes:
time: 504 us; the launch traced here: 495 us
  waiting for transfers between devices  276 us (55%)
  local copies, waits for them, and re-layouts  85.7 us (17%)
  matrix products  71 us (14%)
  starting transfers between devices  29 us (6%)
  other arithmetic  18.5 us (4%)
  between operations  15.1 us (3%)
    psum x1, waiting for transfers between devices, body(): summed = lax.psum(flattened, ('dp', 'rep'))  265 us
    dot_general x32, matrix products, project(): return jnp.einsum('...i,ij->...j', inputs.astype(jnp.float32), matrix)  45.2 us
    reshape x14, local copies, waits for them, and re-layouts, body(): gradient.reshape(dp_count, -1)  17.6 us
    reshape x14, local copies, waits for them, and re-layouts, body(): outputs.append(summed[:, offset:offset + extent].reshape(gradient.shape))  13.3 us
    all_to_all x1, starting transfers between devices, body(): lax.all_to_all(send_ids.reshape(dp_count, slot_count), 'dp', split_axis=0...  12.2 us
    dot_general x6, matrix products, attention(): jnp.einsum('bhlm,bmhd->blhd', weights, value_rows, preferred_element_type...  11.3 us
    all_to_all x1, starting transfers between devices, body(): lax.all_to_all(send_rows.reshape(dp_count, slot_count, feature), 'dp', sp...  11 us
  transfers between devices with their start and end apart: 4, of which 3 were waited for; matrix products, arithmetic and copies ran while one was open for 8% of the time, Pallas kernels for 0%

commit v1 on v0

--- a/solution.py
+++ b/solution.py
@@ -1,14 +1,293 @@
+import functools
 import math
 
 import jax
 import jax.numpy as jnp
 from jax import lax
+from jax.experimental import pallas as pl
+from jax.experimental.pallas import tpu as pltpu
 from jax.sharding import PartitionSpec as P
 
 HEADS = 8
-
-
 EPSILON = 1e-06
+MESH = pl.DeviceIdType.MESH
+F32 = jnp.float32
+BF16 = jnp.bfloat16
+N_DP = 64
+
+
+def place():
+    dp, rep = lax.axis_index("dp"), lax.axis_index("rep")
+    z, x, core = lax.div(dp, 8), lax.rem(lax.div(dp, 2), 4), lax.rem(dp, 2)
+    first = (1 - core) * rep + core * x
+    second = (1 - core) * x + core * rep
+    return dp, rep, z, x, core, first, second
+
+
+def core_peer(at):
+    dp, rep, z, x, core, first, second = at
+    return (dp + 1 - 2 * core, rep)
+
+
+def first_peer(at, j):
+    dp, rep, z, x, core, first, second = at
+    return ((1 - core) * dp + core * (8 * z + 2 * j + core), (1 - core) * j + core * rep)
+
+
+def second_peer(at, j):
+    dp, rep, z, x, core, first, second = at
+    return (core * dp + (1 - core) * (8 * z + 2 * j + core), core * j + (1 - core) * rep)
+
+
+def z_peer(at, j):
+    dp, rep, z, x, core, first, second = at
+    return (8 * j + 2 * x + core, rep)
+
+
+def greet_ring(at, barrier):
+    dp, rep, z, x, core, first, second = at
+    peers = [core_peer(at)]
+    peers += [first_peer(at, lax.rem(first + d, 4)) for d in (1, 2, 3)]
+    peers += [second_peer(at, lax.rem(second + d, 4)) for d in (1, 2, 3)]
+    peers += [z_peer(at, lax.rem(z + d, 8)) for d in range(1, 8)]
+    for peer in peers:
+        pl.semaphore_signal(barrier, inc=1, device_id=peer, device_id_type=MESH)
+    return len(peers)
+
+
+def remote(src, dst, send, recv, peer):
+    copy = pltpu.make_async_remote_copy(
+        src_ref=src, dst_ref=dst, send_sem=send, recv_sem=recv, device_id=peer, device_id_type=MESH
+    )
+    copy.start()
+    return copy
+
+
+class Summing:
+    def __init__(self, at, n, mine, total, scratch):
+        self.at, self.n, self.mine, self.total = at, n, mine, total
+        self.m = -(-2 * n // 8)
+        (self.core_in, self.first_out, self.first_in, self.second_out, self.second_in,
+         self.z_out, self.z_in, self.z_all, self.send, self.recv) = scratch
+        self.copies = []
+
+    @staticmethod
+    def scratch(n):
+        m = -(-2 * n // 8)
+        return [
+            pltpu.VMEM((4, 4, n, 16, 128), BF16),
+            pltpu.VMEM((4, 4, n, 16, 128), BF16),
+            pltpu.VMEM((3, 4, n, 16, 128), BF16),
+            pltpu.VMEM((4, n, 16, 128), BF16),
+            pltpu.VMEM((3, n, 16, 128), BF16),
+            pltpu.VMEM((8, m, 8, 128), F32),
+            pltpu.VMEM((7, m, 8, 128), F32),
+            pltpu.VMEM((8, m, 8, 128), F32),
+            pltpu.SemaphoreType.DMA((34,)),
+            pltpu.SemaphoreType.DMA((34,)),
+        ]
+
+    def _send(self, src, dst, k, peer):
+        copy = remote(src, dst, self.send.at[k], self.recv.at[k], peer)
+        self.copies.append(copy)
+        return copy
+
+    def start(self):
+        dp, rep, z, x, core, first, second = self.at
+        self.from_core = []
+        for k, d in enumerate((1, 2, 3, 0)):
+            q = lax.rem(second + d, 4)
+            self.from_core.append(
+                self._send(self.mine.at[1 - core, q], self.core_in.at[q], k, core_peer(self.at))
+            )
+
+    def scatter_first(self):
+        dp, rep, z, x, core, first, second = self.at
+        self.from_first = []
+        for k, d in enumerate((1, 2, 3, 0)):
+            q = lax.rem(first + d, 4)
+            self.from_core[k].wait_recv()
+            both = self.mine[core, q].astype(F32) + self.core_in[q].astype(F32)
+            self.first_out[q] = both.astype(BF16)
+            if d:
+                self.from_first.append(
+                    self._send(self.first_out.at[q], self.first_in.at[d - 1], 3 + d, first_peer(self.at, q))
+                )
+
+    def scatter_second(self):
+        dp, rep, z, x, core, first, second = self.at
+        for copy in self.from_first:
+            copy.wait_recv()
+        self.from_second = []
+        for d in (1, 2, 3, 0):
+            q = lax.rem(second + d, 4)
+            value = self.first_out[first, q].astype(F32)
+            for i in range(3):
+                value = value + self.first_in[i, q].astype(F32)
+            self.second_out[q] = value.astype(BF16)
+            if d:
+                self.from_second.append(
+                    self._send(self.second_out.at[q], self.second_in.at[d - 1], 6 + d, second_peer(self.at, q))
+                )
+
+    def scatter_z(self):
+        dp, rep, z, x, core, first, second = self.at
+        for copy in self.from_second:
+            copy.wait_recv()
+        value = self.second_out[second].astype(F32)
+        for i in range(3):
+            value = value + self.second_in[i].astype(F32)
+        value = value.reshape(2 * self.n, 8, 128)
+        extra = 8 * self.m - 2 * self.n
+        if extra:
+            value = jnp.concatenate([value, jnp.zeros((extra, 8, 128), F32)], axis=0)
+        self.z_out[...] = value.reshape(8, self.m, 8, 128)
+        self.from_z = []
+        for d in range(1, 8):
+            q = lax.rem(z + d, 8)
+            self.from_z.append(
+                self._send(self.z_out.at[q], self.z_in.at[d - 1], 9 + d, z_peer(self.at, q))
+            )
+
+    def gather_z(self):
+        dp, rep, z, x, core, first, second = self.at
+        for copy in self.from_z:
+            copy.wait_recv()
+        value = self.z_out[z]
+        for i in range(7):
+            value = value + self.z_in[i]
+        self.z_all[z] = value
+        self.from_z = []
+        for d in range(1, 8):
+            q = lax.rem(z + d, 8)
+            self.from_z.append(
+                self._send(self.z_all.at[z], self.z_all.at[z], 16 + d, z_peer(self.at, q))
+            )
+
+    def gather_second(self):
+        dp, rep, z, x, core, first, second = self.at
+        for copy in self.from_z:
+            copy.wait_recv()
+        value = self.z_all[...].reshape(8 * self.m, 8, 128)[: 2 * self.n]
+        self.total[core, first, second] = value.reshape(self.n, 16, 128).astype(BF16)
+        here = self.total.at[core, first, second]
+        self.from_second = []
+        for d in (1, 2, 3):
+            q = lax.rem(second + d, 4)
+            self.from_second.append(self._send(here, here, 23 + d, second_peer(self.at, q)))
+
+    def gather_first(self):
+        dp, rep, z, x, core, first, second = self.at
+        for copy in self.from_second:
+            copy.wait_recv()
+        here = self.total.at[core, first]
+        self.from_first = []
+        for d in (1, 2, 3):
+            q = lax.rem(first + d, 4)
+            self.from_first.append(self._send(here, here, 26 + d, first_peer(self.at, q)))
+        self.from_core = [self._send(here, here, 30, core_peer(self.at))]
+
+    def gather_core(self):
+        dp, rep, z, x, core, first, second = self.at
+        for d, copy in zip((1, 2, 3), self.from_first, strict=True):
+            copy.wait_recv()
+            here = self.total.at[core, lax.rem(first + 4 - d, 4)]
+            self.from_core.append(self._send(here, here, 30 + d, core_peer(self.at)))
+
+    def finish(self):
+        for copy in self.from_core:
+            copy.wait_recv()
+        for copy in self.copies:
+            copy.wait_send()
+
+
+def exchange_start(at, out_ref, in_ref, send, recv):
+    dp, rep = at[:2]
+    in_ref[dp] = out_ref[dp]
+
+    def step(d, carry):
+        j = lax.rem(dp + d, N_DP)
+        remote(out_ref.at[j], in_ref.at[dp], send, recv, (j, rep))
+        return carry
+
+    lax.fori_loop(1, N_DP, step, 0)
+
+
+def exchange_wait(at, out_ref, in_ref, send, recv):
+    rest = pl.ds(0, N_DP - 1)
+    copy = pltpu.make_async_remote_copy(
+        src_ref=out_ref.at[rest], dst_ref=in_ref.at[rest], send_sem=send, recv_sem=recv,
+        device_id=core_peer(at), device_id_type=MESH,
+    )
+    copy.wait_recv()
+    copy.wait_send()
+
+
+def greet_group(at, barrier):
+    dp, rep = at[:2]
+
+    def step(d, carry):
+        pl.semaphore_signal(
+            barrier, inc=1, device_id=(lax.rem(dp + d, N_DP), rep), device_id_type=MESH
+        )
+        return carry
+
+    lax.fori_loop(1, N_DP, step, 0)
+    return N_DP - 1
+
+
+VMEM_LIMIT = 48 * 1024 * 1024
+
+
+def exchange_kernel(out_ref, in_ref, send, recv):
+    at = place()
+    barrier = pltpu.get_barrier_semaphore()
+    pl.semaphore_wait(barrier, greet_group(at, barrier))
+    exchange_start(at, out_ref, in_ref, send, recv)
+    exchange_wait(at, out_ref, in_ref, send, recv)
+
+
+def exchange(rows, collective_id):
+    return pl.pallas_call(
+        exchange_kernel,
+        out_shape=jax.ShapeDtypeStruct(rows.shape, rows.dtype),
+        in_specs=[pl.BlockSpec(memory_space=pltpu.VMEM)],
+        out_specs=pl.BlockSpec(memory_space=pltpu.VMEM),
+        scratch_shapes=[pltpu.SemaphoreType.DMA, pltpu.SemaphoreType.DMA],
+        compiler_params=pltpu.CompilerParams(
+            collective_id=collective_id, has_side_effects=True, vmem_limit_bytes=VMEM_LIMIT
+        ),
+    )(rows)
+
+
+def summing_kernel(n, mine_ref, total_ref, *scratch):
+    at = place()
+    barrier = pltpu.get_barrier_semaphore()
+    pl.semaphore_wait(barrier, greet_ring(at, barrier))
+    job = Summing(at, n, mine_ref, total_ref, scratch)
+    job.start()
+    job.scatter_first()
+    job.scatter_second()
+    job.scatter_z()
+    job.gather_z()
+    job.gather_second()
+    job.gather_first()
+    job.gather_core()
+    job.finish()
+
+
+def summed_over_devices(mine, collective_id):
+    n = mine.shape[3]
+    return pl.pallas_call(
+        functools.partial(summing_kernel, n),
+        out_shape=jax.ShapeDtypeStruct(mine.shape, mine.dtype),
+        in_specs=[pl.BlockSpec(memory_space=pltpu.VMEM)],
+        out_specs=pl.BlockSpec(memory_space=pltpu.VMEM),
+        scratch_shapes=Summing.scratch(n),
+        compiler_params=pltpu.CompilerParams(
+            collective_id=collective_id, has_side_effects=True, vmem_limit_bytes=VMEM_LIMIT
+        ),
+    )(mine)
 
 
 def scaled_norm(values, gain_vec):
@@ -144,19 +423,17 @@
         placing.astype(jnp.bfloat16), embedded, preferred_element_type=jnp.float32
     ).astype(jnp.bfloat16)
     send_ids = jnp.sum(placing.astype(jnp.int32) * (owner_row + 1)[None, :], axis=1)
-    got_rows, got_ids = (
-        lax.all_to_all(
-            send_rows.reshape(dp_count, slot_count, feature),
-            "dp",
-            split_axis=0,
-            concat_axis=0,
-            tiled=True,
-        ),
-        lax.all_to_all(
-            send_ids.reshape(dp_count, slot_count), "dp", split_axis=0, concat_axis=0, tiled=True
-        ),
-    )
-    got_rows = got_rows.reshape(dp_count * slot_count, feature)
+    packed = jnp.concatenate(
+        [
+            send_rows.astype(F32).reshape(dp_count, 4, 128),
+            jnp.broadcast_to(send_ids.astype(F32).reshape(dp_count, 2, 1), (dp_count, 2, 128)),
+            jnp.zeros((dp_count, 2, 128), F32),
+        ],
+        axis=1,
+    )
+    got = exchange(packed, 1)
+    got_rows = got[:, :4].astype(BF16).reshape(dp_count * slot_count, feature)
+    got_ids = got[:, 4:6, 0].astype(jnp.int32)
     member = got_ids.reshape(-1)[None, :] == jnp.arange(1, parent_count + 1)[:, None]
     counts = jnp.sum(member.astype(jnp.float32), axis=1)
     sum_rows = jnp.dot(member.astype(jnp.bfloat16), got_rows, preferred_element_type=jnp.float32)
@@ -171,13 +448,12 @@
     parent_grads, pooled_grad = parent_pullback(cotangent.astype(jnp.float32) * loss_scale)
     sum_grad = pooled_grad.astype(jnp.float32) / divisor
     slot_grad = jnp.dot(member.T.astype(jnp.float32), sum_grad).astype(jnp.bfloat16)
-    returned = lax.all_to_all(
-        slot_grad.reshape(dp_count, slot_count, feature),
-        "dp",
-        split_axis=0,
-        concat_axis=0,
-        tiled=True,
-    )
+    returned = exchange(
+        jnp.concatenate(
+            [slot_grad.astype(F32).reshape(dp_count, 4, 128), jnp.zeros((dp_count, 4, 128), F32)], axis=1
+        ),
+        2,
+    )[:, :4].astype(BF16)
     item_grad = jnp.dot(
         placing.T.astype(jnp.bfloat16),
         returned.reshape(dp_count * slot_count, feature),
@@ -185,14 +461,19 @@
     ).astype(jnp.bfloat16)
     item_grads = item_pullback(item_grad)[0]
     gradients = tuple(item_grads) + tuple(parent_grads)
-    flattened = jnp.concatenate([gradient.reshape(dp_count, -1) for gradient in gradients], axis=1)
-    summed = lax.psum(flattened, ("dp", "rep"))
+    matrices = [gradient for gradient in gradients if gradient.ndim == 2]
+    gains = [gradient for gradient in gradients if gradient.ndim == 1]
+    flattened = jnp.concatenate([gradient.reshape(-1) for gradient in matrices]).astype(BF16)
+    summed = summed_over_devices(flattened.reshape(2, 4, 4, 17, 16, 128), 3).astype(F32).reshape(-1)
+    gain_sums = list(lax.psum(jnp.stack(gains), ("dp", "rep")))
     outputs = []
     offset = 0
     for gradient in gradients:
-        extent = gradient.size // dp_count
-        outputs.append(summed[:, offset : offset + extent].reshape(gradient.shape))
-        offset = offset + extent
+        if gradient.ndim == 1:
+            outputs.append(gain_sums.pop(0))
+            continue
+        outputs.append(summed[offset : offset + gradient.size].reshape(gradient.shape))
+        offset = offset + gradient.size
     return (states.astype(jnp.bfloat16),) + tuple(outputs)
 
 

time: 504 us -> 299 us (0.59)
  the two profiles are of different devices: /device:TPU:2 before, /device:TPU:1 now
where the time goes in v1:
time: 299 us; the launch traced here: 296 us
  Pallas kernels  86 us (29%)
  blocking collectives  74.8 us (25%)
  local copies, waits for them, and re-layouts  63.9 us (21%)
  matrix products  54.8 us (18%)
  other arithmetic  14 us (5%)
    psum x1, blocking collectives, body(): gain_sums = list(lax.psum(jnp.stack(gains), ('dp', 'rep')))  74.8 us
    pallas_call x1, Pallas kernels, summed_over_devices(): pl.pallas_call(functools.partial(summing_kernel, n), out_shape=jax.ShapeD...  51.3 us
    pallas_call x2, Pallas kernels, exchange(): pl.pallas_call(exchange_kernel, out_shape=jax.ShapeDtypeStruct(rows.shape...  34.6 us
    dot_general x32, matrix products, project(): return jnp.einsum('...i,ij->...j', inputs.astype(jnp.float32), matrix)  30.7 us
    unnamed x211, local copies, waits for them, and re-layouts  14.8 us
    slice x5, local copies, waits for them, and re-layouts, body(): summed[offset:offset + gradient.size].reshape(gradient.shape)  13.7 us
    dot_general x6, matrix products, attention(): jnp.einsum('bhlm,bmhd->blhd', weights, value_rows, preferred_element_type...  12 us
    reshape x4, local copies, waits for them, and re-layouts, attention(): key_rows = project(normed, key_matrix).astype(jnp.bfloat16).reshape(row_c...  7.59 us

profile of v1, /device:TPU:1, one launch (start us, length us, event | category | flops | bytes accessed | tf_op | source)
XLA Modules:
  0.0 296.0 jit_solution(555439984016207088)
XLA Ops:
  7.3 7.0 %fusion.179 = (f32[24,8,24]{2,1,0:T(8,128)S(1)}, f32[24,8,24,24]{2,3,1,0:T(8,128)S(1)}) fusion(f32[24,8,24,24]{2,3,1,0:T(8,128)S(1)} %fusion.80), kind=kOutput, calls=%fused_computation.258 | output fusion | flops 442391 | bytes 903168 | tf_op jit(solution)/shard_map/jvp()/sub | solution.py:324
  15.8 2.5 reshape.280
  18.3 2.1 fusion.27
  21.7 2.1 convert_element_type.305
  28.9 19.5 %shard_map.298 = f32[64,8,128]{2,1,0:T(8,128)S(1)} custom-call(f32[64,8,128]{2,1,0:T(8,128)S(1)} %maximum_maximum_fusion.out_ref), custom_call_target="tpu_custom_call" | custom-call | tf_op jit(solution)/shard_map/pallas_call | solution.py:251
  49.2 1.8 convert_reduce_fusion.1
  57.9 1.4 reshape.287
  61.8 3.9 %fusion.180 = (f32[16,8,32]{2,1,0:T(8,128)S(1)}, f32[16,8,32,32]{2,3,1,0:T(8,128)}) fusion(bf16[16,32,8,32]{3,2,1,0:T(8,128)(2,1)} %reshape.288, bf16[16,32,8,32]{3,2,1,0:T(8,128)(2,1)} %reshape.287), kind=kOutput, calls=%fused_computation.259 | convolution fusion | flops 8781855 | bytes 1064960 | tf_op jit(solution)/shard_map/jvp()/sub | solution.py:324
  71.5 3.0 %fusion.20 = (f32[16,8,32]{2,1,0:T(8,128)S(1)}, bf16[16,8,32,32]{2,3,1,0:T(8,128)(2,1)S(1)}) fusion(f32[16,8,32,32]{2,3,1,0:T(8,128)} %get-tuple-element.36, f32[16,8,32]{2,1,0:T(8,128)} %multiply_divide_fusion.1, bf16[16,8,32,32]{3,2,1,0:T(8,128)(2,1)} %bitcast.231, bf16[16,32,8,32]{3,2,1,0:T(8,128)(2,1)} %reshape.286), kind=kOutput, calls=%fused_computation.31 | convolution fusion | flops 9039872 | bytes 1343488 | tf_op jit(solution)/shard_map/transpose(jvp(bhlm,bmhd->blhd))/dot_general | solution.py:325
  75.6 1.4 copy.101
  77.0 2.8 reshape.291
  79.8 2.7 convolution_convert_fusion.9
  85.4 1.4 copy.104
  86.8 2.0 reshape.292
  90.2 1.5 fusion.101
  92.8 1.7 convolution_convert_fusion.27
  95.4 15.1 %shard_map.299 = f32[64,8,128]{2,1,0:T(8,128)S(1)} custom-call(f32[64,8,128]{2,1,0:T(8,128)S(1)} %pad_convert_fusion.out_ref), custom_call_target="tpu_custom_call" | custom-call | tf_op jit(solution)/shard_map/pallas_call | solution.py:251
  111.4 3.7 %fusion.3 = bf16[24,24,1024]{2,1,0:T(8,128)(2,1)S(1)} fusion(f32[24,24,1024]{2,1,0:T(8,128)} %copy-done.15, bf16[1024,256]{1,0:T(8,128)(2,1)} %param.31, bf16[24,256]{1,0:T(8,128)(2,1)S(1)} %fusion.70), kind=kOutput, calls=%fused_computation.11 | convolution fusion | flops 314376192 | bytes 4075520 | tf_op jit(solution)/shard_map/transpose(jvp(...i,ij->...j))/dot_general | solution.py:299
  119.2 2.5 reshape.295
  121.7 2.8 fusion.10
  127.0 2.9 reshape.297
  129.9 1.5 fusion.63
  137.8 2.8 reshape.296
  140.6 1.4 fusion.62
  151.4 1.6 copy-done.3
  153.0 51.3 %shard_map.300 = bf16[2,4,4,17,16,128]{5,4,3,2,1,0:T(8,128)(2,1)S(1)} custom-call(bf16[2,4,4,17,16,128]{5,4,3,2,1,0:T(8,128)(2,1)S(1)} %bitcast.230), custom_call_target="tpu_custom_call" | custom-call | tf_op jit(solution)/shard_map/pallas_call | solution.py:281
  204.3 3.0 %slice.62 = f32[4352,256]{1,0:T(8,128)} reshape(bf16[2,4,4,17,16,128]{5,4,3,2,1,0:T(8,128)(2,1)S(1)} %shard_map.300) | data formatting | bytes 6684672 | tf_op jit(solution)/shard_map/slice | solution.py:475
  207.3 3.0 %fusion.177 = (f32[256,256]{1,0:T(8,128)}, f32[256,256]{1,0:T(8,128)}, f32[256,256]{1,0:T(8,128)}, f32[256,256]{1,0:T(8,128)}, f32[256,256]{1,0:T(8,128)}, /*ind...) fusion(f32[4352,256]{1,0:T(8,128)} %slice.62), kind=kLoop, calls=%fused_computation.256 | loop fusion | bytes 4718592 | tf_op jit(solution)/shard_map/slice | solution.py:475
  210.3 2.9 slice.67
  213.2 2.4 slice.81
  215.7 2.4 slice.82
  219.1 74.8 %psum.7 = f32[3,256]{1,0:T(4,128)S(1)} all-reduce(f32[3,256]{1,0:T(4,128)S(1)} %pad_maximum_fusion), channel_id=1, replica_groups=mesh['dp'=64,'rep'=4] {'dp','rep'}, use_global_device_ids=true, to_apply=%region_19.0 | all-reduce | flops 768 | bytes 6144 | tf_op jit(solution)/shard_map/psum | solution.py:468
  (297 shorter events, 62.3 us)
Async XLA Ops:
  0.6 25.2 %copy-start = (bf16[256,1024]{1,0:T(8,128)(2,1)S(1)}, bf16[256,1024]{1,0:T(8,128)(2,1)}, u32[]{:S(2)}) copy-start(bf16[256,1024]{1,0:T(8,128)(2,1)} %param.30) | copy-start | bytes 1572868
  0.7 3.7 %copy-start.21 = (bf16[24,24,256]{2,1,0:T(8,128)(2,1)S(1)}, bf16[24,24,256]{2,1,0:T(8,128)(2,1)}, u32[]{:S(2)}) copy-start(bf16[24,24,256]{2,1,0:T(8,128)(2,1)} %param.19) | copy-start | bytes 884740
  1.9 12.5 %copy-start.73 = (f32[24,24]{1,0:T(8,128)}, f32[24,24]{1,0:T(8,128)S(1)}, u32[]{:S(2)}) copy-start(f32[24,24]{1,0:T(8,128)S(1)} %add_rsqrt_fusion) | copy-start | bytes 6916
  2.6 11.9 %copy-start.93 = (f32[256]{0:T(256)}, f32[256]{0:T(256)S(1)}, u32[]{:S(2)}) copy-start(f32[256]{0:T(256)S(1)} %convert_element_type.297) | copy-start | bytes 3076
  7.3 7.1 %copy-start.90 = (bf16[256,256]{1,0:T(8,128)(2,1)S(1)}, bf16[256,256]{1,0:T(8,128)(2,1)}, u32[]{:S(2)}) copy-start(bf16[256,256]{1,0:T(8,128)(2,1)} %param.27) | copy-start | bytes 393220
  14.4 6.0 %copy-start.50 = (f32[24,8,24]{2,1,0:T(8,128)}, f32[24,8,24]{2,1,0:T(8,128)S(1)}, u32[]{:S(2)}) copy-start(f32[24,8,24]{2,1,0:T(8,128)S(1)} %get-tuple-element.31) | copy-start | bytes 55300
  14.4 117.2 %copy-start.4 = (f32[24,8,24,24]{2,3,1,0:T(8,128)}, f32[24,8,24,24]{2,3,1,0:T(8,128)S(1)}, u32[]{:S(2)}) copy-start(f32[24,8,24,24]{2,3,1,0:T(8,128)S(1)} %get-tuple-element.32) | copy-start | bytes 1327108
  20.4 5.4 %copy-start.92 = (bf16[256]{0:T(256)(128)(2,1)S(1)}, bf16[256]{0:T(256)(128)(2,1)}, u32[]{:S(2)}) copy-start(bf16[256]{0:T(256)(128)(2,1)} %param.29) | copy-start | bytes 1540
  27.8 26.9 %copy-start.14 = (bf16[16,32,256]{2,1,0:T(8,128)(2,1)S(1)}, bf16[16,32,256]{2,1,0:T(8,128)(2,1)}, u32[]{:S(2)}) copy-start(bf16[16,32,256]{2,1,0:T(8,128)(2,1)} %param.22) | copy-start | bytes 786436
  49.2 10.2 %copy-start.53 = (bf16[256,256]{1,0:T(8,128)(2,1)S(1)}, bf16[256,256]{1,0:T(8,128)(2,1)}, u32[]{:S(2)}) copy-start(bf16[256,256]{1,0:T(8,128)(2,1)} %param.35) | copy-start | bytes 393220
  79.8 3.8 %copy-start.57 = (bf16[256,256]{1,0:T(8,128)(2,1)S(1)}, bf16[256,256]{1,0:T(8,128)(2,1)}, u32[]{:S(2)}) copy-start(bf16[256,256]{1,0:T(8,128)(2,1)} %param.36) | copy-start | bytes 393220
  79.8 4.9 %copy-start.19 = (f32[16,8,32,32]{2,3,1,0:T(8,128)S(1)}, f32[16,8,32,32]{2,3,1,0:T(8,128)}, u32[]{:S(2)}) copy-start(f32[16,8,32,32]{2,3,1,0:T(8,128)} %get-tuple-element.36) | copy-start | bytes 1572868
  79.8 4.9 %copy-start.33 = (bf16[16,32,8,32]{3,2,1,0:T(8,128)(2,1)S(1)}, bf16[16,32,8,32]{3,2,1,0:T(8,128)(2,1)}, u32[]{:S(2)}) copy-start(bf16[16,32,8,32]{3,2,1,0:T(8,128)(2,1)} %reshape.288) | copy-start | bytes 786436
  79.8 4.9 %copy-start.45 = (bf16[16,8,32,32]{2,3,1,0:T(8,128)(2,1)S(1)}, bf16[16,8,32,32]{2,3,1,0:T(8,128)(2,1)}, u32[]{:S(2)}) copy-start(bf16[16,8,32,32]{2,3,1,0:T(8,128)(2,1)} %copy-done.44) | copy-start | bytes 786436
  86.8 6.0 %copy-start.46 = (bf16[256,256]{1,0:T(8,128)(2,1)S(1)}, bf16[256,256]{1,0:T(8,128)(2,1)}, u32[]{:S(2)}) copy-start(bf16[256,256]{1,0:T(8,128)(2,1)} %param.32) | copy-start | bytes 393220
  88.9 21.6 %copy-start.35 = (bf16[16,32,256]{2,1,0:T(8,128)(2,1)}, bf16[16,32,256]{2,1,0:T(8,128)(2,1)S(1)}, u32[]{:S(2)}) copy-start(bf16[16,32,256]{2,1,0:T(8,128)(2,1)S(1)} %reshape.292) | copy-start | bytes 786436
  111.4 3.7 %copy-start.7 = (f32[24,24,256]{2,1,0:T(8,128)S(1)}, f32[24,24,256]{2,1,0:T(8,128)}, u32[]{:S(2)}) copy-start(f32[24,24,256]{2,1,0:T(8,128)} %copy-done.6) | copy-start | bytes 1769476
  111.4 3.7 %copy-start.59 = (f32[24,24]{1,0:T(8,128)S(1)}, f32[24,24]{1,0:T(8,128)}, u32[]{:S(2)}) copy-start(f32[24,24]{1,0:T(8,128)} %copy-done.58) | copy-start | bytes 6916
  111.4 3.7 %copy-start.77 = (f32[256]{0:T(256)S(1)}, f32[256]{0:T(256)}, u32[]{:S(2)}) copy-start(f32[256]{0:T(256)} %copy-done.76) | copy-start | bytes 3076
  117.9 3.8 %copy-start.51 = (f32[24,8,24]{2,1,0:T(8,128)S(1)}, f32[24,8,24]{2,1,0:T(8,128)}, u32[]{:S(2)}) copy-start(f32[24,8,24]{2,1,0:T(8,128)} %copy-done.50) | copy-start | bytes 55300
  118.1 6.4 %copy-start.24 = (bf16[24,24,256]{2,1,0:T(8,128)(2,1)}, bf16[24,24,256]{2,1,0:T(8,128)(2,1)S(1)}, u32[]{:S(2)}) copy-start(bf16[24,24,256]{2,1,0:T(8,128)(2,1)S(1)} %fusion.108) | copy-start | bytes 884740
  125.6 4.3 %copy-start.22 = (bf16[24,24,256]{2,1,0:T(8,128)(2,1)S(1)}, bf16[24,24,256]{2,1,0:T(8,128)(2,1)}, u32[]{:S(2)}) copy-start(bf16[24,24,256]{2,1,0:T(8,128)(2,1)} %param.19) | copy-start | bytes 884740
  125.6 4.3 %copy-start.74 = (f32[24,24]{1,0:T(8,128)S(1)}, f32[24,24]{1,0:T(8,128)}, u32[]{:S(2)}) copy-start(f32[24,24]{1,0:T(8,128)} %copy-done.73) | copy-start | bytes 6916
  125.6 4.3 %copy-start.94 = (f32[256]{0:T(256)S(1)}, f32[256]{0:T(256)}, u32[]{:S(2)}) copy-start(f32[256]{0:T(256)} %copy-done.93) | copy-start | bytes 3076
  137.8 4.3 %copy-start.25 = (bf16[24,24,256]{2,1,0:T(8,128)(2,1)S(1)}, bf16[24,24,256]{2,1,0:T(8,128)(2,1)}, u32[]{:S(2)}) copy-start(bf16[24,24,256]{2,1,0:T(8,128)(2,1)} %copy-done.24) | copy-start | bytes 884740
  213.2 4.9 %copy-start.28 = (bf16[24,24,256]{2,1,0:T(8,128)(2,1)S(1)}, bf16[24,24,256]{2,1,0:T(8,128)(2,1)}, u32[]{:S(2)}) copy-start(bf16[24,24,256]{2,1,0:T(8,128)(2,1)} %reshape.297) | copy-start | bytes 884740
  213.2 4.9 %copy-start.55 = (bf16[256,256]{1,0:T(8,128)(2,1)S(1)}, bf16[256,256]{1,0:T(8,128)(2,1)}, u32[]{:S(2)}) copy-start(bf16[256,256]{1,0:T(8,128)(2,1)} %param.26) | copy-start | bytes 393220
  213.2 5.2 %copy-start.30 = (bf16[24,24,256]{2,1,0:T(8,128)(2,1)S(1)}, bf16[24,24,256]{2,1,0:T(8,128)(2,1)}, u32[]{:S(2)}) copy-start(bf16[24,24,256]{2,1,0:T(8,128)(2,1)} %copy-done.29) | copy-start | bytes 884740
  213.2 5.2 %copy-start.56 = (bf16[256,256]{1,0:T(8,128)(2,1)S(1)}, bf16[256,256]{1,0:T(8,128)(2,1)}, u32[]{:S(2)}) copy-start(bf16[256,256]{1,0:T(8,128)(2,1)} %param.25) | copy-start | bytes 393220
  215.7 78.9 %copy-start.40 = (bf16[16,8,32,32]{3,2,1,0:T(8,128)(2,1)S(1)}, bf16[16,8,32,32]{3,2,1,0:T(8,128)(2,1)}, u32[]{:S(2)}) copy-start(bf16[16,8,32,32]{3,2,1,0:T(8,128)(2,1)} %copy-done.39) | copy-start | bytes 786436
  215.7 78.9 %copy-start.49 = (bf16[256,256]{1,0:T(8,128)(2,1)S(1)}, bf16[256,256]{1,0:T(8,128)(2,1)}, u32[]{:S(2)}) copy-start(bf16[256,256]{1,0:T(8,128)(2,1)} %param.37) | copy-start | bytes 393220
  215.7 80.0 %copy-start.1 = (bf16[256,1024]{1,0:T(8,128)(2,1)S(1)}, bf16[256,1024]{1,0:T(8,128)(2,1)}, u32[]{:S(2)}) copy-start(bf16[256,1024]{1,0:T(8,128)(2,1)} %param.30) | copy-start | bytes 1572868
  (63 other events, 118.9 us)

commit v2 on v1

v2 whole, which is shorter than its diff:
```python
import math

import jax
import jax.numpy as jnp
from jax import lax
from jax.experimental import pallas as pl
from jax.experimental.pallas import tpu as pltpu
from jax.sharding import PartitionSpec as P

MESH = pl.DeviceIdType.MESH
F32 = jnp.float32
BF16 = jnp.bfloat16
N_DP = 64


def place():
    dp, rep = lax.axis_index("dp"), lax.axis_index("rep")
    z, x, core = lax.div(dp, 8), lax.rem(lax.div(dp, 2), 4), lax.rem(dp, 2)
    first = (1 - core) * rep + core * x
    second = (1 - core) * x + core * rep
    return dp, rep, z, x, core, first, second


def core_peer(at):
    dp, rep, z, x, core, first, second = at
    return (dp + 1 - 2 * core, rep)


def first_peer(at, j):
    dp, rep, z, x, core, first, second = at
    return ((1 - core) * dp + core * (8 * z + 2 * j + core), (1 - core) * j + core * rep)


def second_peer(at, j):
    dp, rep, z, x, core, first, second = at
    return (core * dp + (1 - core) * (8 * z + 2 * j + core), core * j + (1 - core) * rep)


def z_peer(at, j):
    dp, rep, z, x, core, first, second = at
    return (8 * j + 2 * x + core, rep)


def remote(src, dst, send, recv, peer):
    copy = pltpu.make_async_remote_copy(
        src_ref=src, dst_ref=dst, send_sem=send, recv_sem=recv, device_id=peer, device_id_type=MESH
    )
    copy.start()
    return copy


class Summing:
    def __init__(self, at, n, mine, total, scratch):
        self.at, self.n, self.mine, self.total = at, n, mine, total
        self.m = -(-2 * n // 8)
        (self.core_in, self.first_out, self.first_in, self.second_out, self.second_in,
         self.z_out, self.z_in, self.z_all, self.send, self.recv) = scratch
        self.copies = []

    @staticmethod
    def scratch(n):
        m = -(-2 * n // 8)
        return [
            pltpu.VMEM((4, 4, n, 16, 128), BF16),
            pltpu.VMEM((4, 4, n, 16, 128), BF16),
            pltpu.VMEM((3, 4, n, 16, 128), BF16),
            pltpu.VMEM((4, n, 16, 128), BF16),
            pltpu.VMEM((3, n, 16, 128), BF16),
            pltpu.VMEM((8, m, 8, 128), F32),
            pltpu.VMEM((7, m, 8, 128), F32),
            pltpu.VMEM((8, m, 8, 128), F32),
            pltpu.SemaphoreType.DMA((34,)),
            pltpu.SemaphoreType.DMA((34,)),
        ]

    def _send(self, src, dst, k, peer):
        copy = remote(src, dst, self.send.at[k], self.recv.at[k], peer)
        self.copies.append(copy)
        return copy

    def start(self):
        dp, rep, z, x, core, first, second = self.at
        self.from_core = []
        for k, d in enumerate((1, 2, 3, 0)):
            q = lax.rem(second + d, 4)
            self.from_core.append(
                self._send(self.mine.at[1 - core, q], self.core_in.at[q], k, core_peer(self.at))
            )

    def scatter_first(self):
        dp, rep, z, x, core, first, second = self.at
        self.from_first = []
        for k, d in enumerate((1, 2, 3, 0)):
            q = lax.rem(first + d, 4)
            self.from_core[k].wait_recv()
            both = self.mine[core, q].astype(F32) + self.core_in[q].astype(F32)
            self.first_out[q] = both.astype(BF16)
            if d:
                self.from_first.append(
                    self._send(self.first_out.at[q], self.first_in.at[d - 1], 3 + d, first_peer(self.at, q))
                )

    def scatter_second(self):
        dp, rep, z, x, core, first, second = self.at
        for copy in self.from_first:
            copy.wait_recv()
        self.from_second = []
        for d in (1, 2, 3, 0):
            q = lax.rem(second + d, 4)
            value = self.first_out[first, q].astype(F32)
            for i in range(3):
                value = value + self.first_in[i, q].astype(F32)
            self.second_out[q] = value.astype(BF16)
            if d:
                self.from_second.append(
                    self._send(self.second_out.at[q], self.second_in.at[d - 1], 6 + d, second_peer(self.at, q))
                )

    def scatter_z(self):
        dp, rep, z, x, core, first, second = self.at
        for copy in self.from_second:
            copy.wait_recv()
        value = self.second_out[second].astype(F32)
        for i in range(3):
            value = value + self.second_in[i].astype(F32)
        value = value.reshape(2 * self.n, 8, 128)
        extra = 8 * self.m - 2 * self.n
        if extra:
            value = jnp.concatenate([value, jnp.zeros((extra, 8, 128), F32)], axis=0)
        self.z_out[...] = value.reshape(8, self.m, 8, 128)
        self.from_z = []
        for d in range(1, 8):
            q = lax.rem(z + d, 8)
            self.from_z.append(
                self._send(self.z_out.at[q], self.z_in.at[d - 1], 9 + d, z_peer(self.at, q))
            )

    def gather_z(self):
        dp, rep, z, x, core, first, second = self.at
        for copy in self.from_z:
            copy.wait_recv()
        value = self.z_out[z]
        for i in range(7):
            value = value + self.z_in[i]
        self.z_all[z] = value
        self.from_z = []
        for d in range(1, 8):
            q = lax.rem(z + d, 8)
            self.from_z.append(
                self._send(self.z_all.at[z], self.z_all.at[z], 16 + d, z_peer(self.at, q))
            )

    def gather_second(self):
        dp, rep, z, x, core, first, second = self.at
        for copy in self.from_z:
            copy.wait_recv()
        value = self.z_all[...].reshape(8 * self.m, 8, 128)[: 2 * self.n]
        self.total[core, first, second] = value.reshape(self.n, 16, 128).astype(BF16)
        here = self.total.at[core, first, second]
        self.from_second = []
        for d in (1, 2, 3):
            q = lax.rem(second + d, 4)
            self.from_second.append(self._send(here, here, 23 + d, second_peer(self.at, q)))

    def gather_first(self):
        dp, rep, z, x, core, first, second = self.at
        for copy in self.from_second:
            copy.wait_recv()
        here = self.total.at[core, first]
        self.from_first = []
        for d in (1, 2, 3):
            q = lax.rem(first + d, 4)
            self.from_first.append(self._send(here, here, 26 + d, first_peer(self.at, q)))
        self.from_core = [self._send(here, here, 30, core_peer(self.at))]

    def gather_core(self):
        dp, rep, z, x, core, first, second = self.at
        for d, copy in zip((1, 2, 3), self.from_first, strict=True):
            copy.wait_recv()
            here = self.total.at[core, lax.rem(first + 4 - d, 4)]
            self.from_core.append(self._send(here, here, 30 + d, core_peer(self.at)))

    def finish(self):
        for copy in self.from_core:
            copy.wait_recv()
        for copy in self.copies:
            copy.wait_send()


def exchange_start(at, out_ref, in_ref, send, recv):
    dp, rep = at[:2]
    in_ref[dp] = out_ref[dp]

    def to(d):
        j = lax.rem(dp + d, N_DP)
        remote(out_ref.at[j], in_ref.at[dp], send, recv, (j, rep))

    def step(d, carry):
        to(N_DP // 2 - d)
        to(N_DP // 2 + d)
        return carry

    to(N_DP // 2)
    lax.fori_loop(1, N_DP // 2, step, 0)


def exchange_wait(at, out_ref, in_ref, send, recv):
    rest = pl.ds(0, N_DP - 1)
    copy = pltpu.make_async_remote_copy(
        src_ref=out_ref.at[rest], dst_ref=in_ref.at[rest], send_sem=send, recv_sem=recv,
        device_id=core_peer(at), device_id_type=MESH,
    )
    copy.wait_recv()
    copy.wait_send()


def greet_all(at, barrier):
    dp, rep = at[:2]

    def step(d, carry):
        pl.semaphore_signal(
            barrier, inc=1, device_id=(lax.rem(dp + d, N_DP), rep), device_id_type=MESH
        )
        return carry

    lax.fori_loop(1, N_DP, step, 0)
    for d in (1, 2, 3):
        pl.semaphore_signal(
            barrier, inc=1, device_id=(dp, lax.rem(rep + d, 4)), device_id_type=MESH
        )
    return N_DP + 2


VMEM_LIMIT = 56 * 1024 * 1024
EPSILON = 1e-06
HEADS = 8
W = 256
HEAD = 32
FF = 1024
TX, COLS = 24, 24
CUST, CTOK = 16, 32
ROWS = TX * COLS
PROWS = CUST * CTOK
GROUP = 4
GROWS = GROUP * COLS
GPROWS = GROUP * CTOK
GROUPS = TX // GROUP
PGROUPS = CUST // GROUP


def dot(a, b):
    return lax.dot_general(a, b, (((1,), (0,)), ((), ())), preferred_element_type=F32)


def dot_nt(a, b):
    return lax.dot_general(a, b, (((1,), (1,)), ((), ())), preferred_element_type=F32)


def dot_tn(a, b):
    return lax.dot_general(a, b, (((0,), (0,)), ((), ())), preferred_element_type=F32)


def each(count, step, body, unroll=1):
    def one(i, carry):
        body(pl.ds(pl.multiple_of(i * step, step), step), i)
        return carry

    lax.fori_loop(0, count, one, 0, unroll=unroll)


def head_masks():
    lane = lax.broadcasted_iota(jnp.int32, (1, W), 1)
    return [jnp.where(lax.div(lane, HEAD) == h, 1.0, 0.0) for h in range(HEADS)]


def spread_heads(value, masks):
    return jnp.concatenate([value * mask.astype(BF16) for mask in masks], axis=0)


def join_heads(value, masks, rows):
    total = value[:rows] * masks[0]
    for h in range(1, HEADS):
        total = total + value[h * rows : (h + 1) * rows] * masks[h]
    return total


def same_owner(rows, length):
    i = lax.div(lax.broadcasted_iota(jnp.int32, (rows, rows), 0), length)
    j = lax.div(lax.broadcasted_iota(jnp.int32, (rows, rows), 1), length)
    return jnp.concatenate([jnp.where(i == j, 0.0, -1e30)] * HEADS, axis=0)


def attend(q, k, v, probs, mix, groups, rows, length):
    masks = head_masks()
    bias = same_owner(rows, length)

    def body(at, i):
        wide = spread_heads(q[at], masks)
        scores = dot_nt(wide, k[at]) * HEAD**-0.5 + bias
        e = jnp.exp(scores - jnp.max(scores, axis=1, keepdims=True))
        p = (e * (1.0 / jnp.sum(e, axis=1, keepdims=True))).astype(BF16)
        probs[i] = p
        mix[at] = join_heads(dot(p, v[at]), masks, rows).astype(BF16)

    each(groups, rows, body)


def attend_back(q, k, v, probs, dmix, dqkv, groups, rows):
    masks = head_masks()

    def body(at, i):
        p = probs[i]
        wide_d = spread_heads(dmix[at], masks)
        wide_q = spread_heads(q[at], masks)
        dp = dot_nt(wide_d, v[at]).astype(BF16).astype(F32)
        weighted = p.astype(F32)
        ds = weighted * (dp - jnp.sum(weighted * dp, axis=1, keepdims=True))
        ds = (ds * HEAD**-0.5).astype(BF16)
        dqkv[at, 0:W] = join_heads(dot(ds, k[at]), masks, rows).astype(BF16)
        dqkv[at, W : 2 * W] = dot_tn(ds, wide_q).astype(BF16)
        dqkv[at, 2 * W : 3 * W] = dot_tn(p, wide_d).astype(BF16)

    each(groups, rows, body)


def put_block(mine, b, value):
    for half in range(2):
        part = value[:, half * 128 : (half + 1) * 128].astype(BF16)
        mine[half, :, :, b] = part.reshape(4, 4, 16, 128)


def rms_scale(value):
    return lax.rsqrt(jnp.mean(value * value, axis=1, keepdims=True) + EPSILON)


def averaging():
    t = lax.broadcasted_iota(jnp.int32, (TX, ROWS), 0)
    r = lax.div(lax.broadcasted_iota(jnp.int32, (TX, ROWS), 1), COLS)
    return jnp.where(t == r, 1.0, 0.0).astype(BF16)


def placing(owner_ref):
    owner = owner_ref[...]
    i = lax.broadcasted_iota(jnp.int32, (TX, TX), 0)
    j = lax.broadcasted_iota(jnp.int32, (TX, TX), 1)
    along = jnp.broadcast_to(owner, (TX, TX))
    down = jnp.sum(jnp.where(i == j, along, 0), axis=1, keepdims=True)
    slot = jnp.sum(jnp.where((down == along) & (i < j), 1, 0), axis=0, keepdims=True)
    device = lax.broadcasted_iota(jnp.int32, (N_DP, TX), 0)
    goes = device == jnp.broadcast_to(owner, (N_DP, TX))
    return [
        jnp.where(goes & (jnp.broadcast_to(slot, (N_DP, TX)) == s), 1.0, 0.0).astype(BF16)
        for s in range(2)
    ]


def encoder_kernel(
    item_ref, owner_ref, row_ref, parent_ref, cot_ref,
    cgain, cq, ck, cv, co, hgain, up, down, link, pgain, pq, pk, pv, po,
    states_ref, parent_sum, mlp_sum, att_sum,
    n1, q, k, v, probs, mix, s_, n2, u, h, slope, dn2, da, dmix, dqkv, hmean,
    pbased, pn, pq_, pk_, pv_, pprobs, pmix, pda, pdmix, pdqkv, pdn,
    parent_mine, mlp_mine, att_mine,
    out1, in1, out2, in2, x_send, x_recv,
    *job_scratch,
):
    at = place()
    barrier = pltpu.get_barrier_semaphore()
    greeted = greet_all(at, barrier)
    per = len(job_scratch) // 3
    parent_job = Summing(at, 5, parent_mine, parent_sum, job_scratch[:per])
    mlp_job = Summing(at, 8, mlp_mine, mlp_sum, job_scratch[per : 2 * per])
    att_job = Summing(at, 4, att_mine, att_sum, job_scratch[2 * per :])

    def norm_items(rows, i):
        x = item_ref[pl.ds(i * GROUP, GROUP)].astype(F32).reshape(GROWS, W)
        n1[rows] = (x * rms_scale(x) * cgain[...].astype(F32)).astype(BF16)

    each(GROUPS, GROWS, norm_items, unroll=2)
    q[...] = dot(n1[...], cq[...]).astype(BF16)
    k[...] = dot(n1[...], ck[...]).astype(BF16)
    v[...] = dot(n1[...], cv[...]).astype(BF16)
    attend(q, k, v, probs, mix, GROUPS, GROWS, COLS)
    u[:, :W] = dot(mix[...], co[...])

    def norm_stream(rows, i):
        x = item_ref[pl.ds(i * GROUP, GROUP)].astype(F32).reshape(GROWS, W)
        stream = (x + u[rows, :W]).astype(BF16)
        s_[rows] = stream
        stream = stream.astype(F32)
        n2[rows] = (stream * rms_scale(stream) * hgain[...].astype(F32)).astype(BF16)

    each(GROUPS, GROWS, norm_stream, unroll=2)
    u[...] = dot(n2[...], up[...])

    def gelu(rows, i):
        for c in range(0, FF, 256):
            value = u[rows, c : c + 256]
            square = value * value
            t = jnp.tanh(math.sqrt(2.0 / math.pi) * value * (1.0 + 0.044715 * square))
            half = 0.5 * (1.0 + t)
            h[rows, c : c + 256] = (value * half).astype(BF16)
            inner = math.sqrt(2.0 / math.pi) * (1.0 + 3 * 0.044715 * square)
            slope[rows, c : c + 256] = (half + 0.5 * value * (1.0 - t * t) * inner).astype(BF16)

    each(ROWS // 32, 32, gelu)
    average = averaging()
    hidden = (dot(average, h[...]) * (1.0 / COLS)).astype(BF16)
    hmean[...] = hidden
    embedding = (dot(average, s_[...]) * (1.0 / COLS) + dot(hidden, down[...])).astype(BF16)

    places = placing(owner_ref)
    ids = jnp.broadcast_to(row_ref[...].astype(F32) + 1.0, (128, TX)).astype(BF16)
    for slot in range(2):
        moved = dot(places[slot], embedding)
        out1[:, 2 * slot, :] = moved[:, :128]
        out1[:, 2 * slot + 1, :] = moved[:, 128:]
        out1[:, 4 + slot, :] = dot_nt(places[slot], ids)
        out1[:, 6 + slot, :] = jnp.zeros((N_DP, 128), F32)
    pl.semaphore_wait(barrier, greeted)
    exchange_start(at, out1, in1, x_send.at[0], x_recv.at[0])
    exchange_wait(at, out1, in1, x_send.at[0], x_recv.at[0])

    members = []
    customer = lax.broadcasted_iota(jnp.int32, (N_DP, CUST), 1).astype(F32) + 1.0
    counts, sums = jnp.zeros((CUST, W), F32), jnp.zeros((CUST, W), F32)
    for slot in range(2):
        got = jnp.concatenate([in1[:, 2 * slot, :], in1[:, 2 * slot + 1, :]], axis=1).astype(BF16)
        member = jnp.where(in1[:, 4 + slot, :][:, :CUST] == customer, 1.0, 0.0).astype(BF16)
        members.append(member)
        counts = counts + dot_tn(member, jnp.ones((N_DP, W), BF16))
        sums = sums + dot_tn(member, got)
    divisor = jnp.maximum(counts, 1.0)
    pooled = (sums / divisor).astype(BF16)
    linked = dot(pooled, link[...])
    scale = 1.0 / math.sqrt(CUST * CTOK * 256)
    pbased_value = (
        (parent_ref[...].astype(F32).reshape(CUST, CTOK, W) + linked[:, None, :])
        .astype(BF16)
        .reshape(PROWS, W)
    )
    pbased[...] = pbased_value

    def norm_based(rows, i):
        x = pbased[rows].astype(F32)
        pn[rows] = (x * rms_scale(x) * pgain[...].astype(F32)).astype(BF16)
        pda[rows] = (cot_ref[rows].astype(F32) * scale).astype(BF16)

    each(PGROUPS, GPROWS, norm_based, unroll=2)
    pq_[...] = dot(pn[...], pq[...]).astype(BF16)
    pk_[...] = dot(pn[...], pk[...]).astype(BF16)
    pv_[...] = dot(pn[...], pv[...]).astype(BF16)
    pdmix[...] = dot_nt(pda[...], po[...]).astype(BF16)
    attend(pq_, pk_, pv_, pprobs, pmix, PGROUPS, GPROWS, CTOK)
    attend_back(pq_, pk_, pv_, pprobs, pdmix, pdqkv, PGROUPS, GPROWS)
    pdn[...] = (
        dot_nt(pdqkv[:, :W], pq[...])
        + dot_nt(pdqkv[:, W : 2 * W], pk[...])
        + dot_nt(pdqkv[:, 2 * W :], pv[...])
    )

    dlinked = []
    for i in range(PGROUPS):
        rows = slice(i * GPROWS, (i + 1) * GPROWS)
        x = pbased[rows].astype(F32)
        r = rms_scale(x)
        unit = x * r
        dunit = pdn[rows] * pgain[...].astype(F32)
        dx = r * (dunit - unit * jnp.mean(dunit * unit, axis=1, keepdims=True))
        dx = dx + cot_ref[rows].astype(F32) * scale
        dlinked.append(jnp.sum(dx.reshape(GROUP, CTOK, W), axis=1))
    dlinked = jnp.concatenate(dlinked, axis=0)
    dpooled = dot_nt(dlinked.astype(BF16), link[...]).astype(BF16).astype(F32)
    sum_grad = (dpooled / divisor).astype(BF16)
    for slot in range(2):
        moved = dot(members[slot], sum_grad)
        out2[:, 2 * slot, :] = moved[:, :128]
        out2[:, 2 * slot + 1, :] = moved[:, 128:]
        out2[:, 4 + slot, :] = jnp.zeros((N_DP, 128), F32)
        out2[:, 6 + slot, :] = jnp.zeros((N_DP, 128), F32)
    exchange_start(at, out2, in2, x_send.at[1], x_recv.at[1])

    put_block(parent_mine, 0, dot_tn(pooled, dlinked.astype(BF16)))
    dweights = dot_tn(pn[...], pdqkv[...])
    for b in range(3):
        put_block(parent_mine, 1 + b, dweights[:, b * W : (b + 1) * W])
    put_block(parent_mine, 4, dot_tn(pmix[...], pda[...]))
    parent_job.start()
    states_ref[...] = (pbased[...].astype(F32) + dot(pmix[...], po[...])).astype(BF16)
    exchange_wait(at, out2, in2, x_send.at[1], x_recv.at[1])

    ditem = jnp.zeros((TX, W), F32)
    for slot in range(2):
        got = jnp.concatenate([in2[:, 2 * slot, :], in2[:, 2 * slot + 1, :]], axis=1).astype(BF16)
        ditem = ditem + dot_tn(places[slot], got)
    ditem_b = ditem.astype(BF16)
    dhidden = (dot_nt(ditem_b, down[...]) * (1.0 / COLS)).astype(BF16)

    spread = averaging()
    u[...] = dot_tn(spread, dhidden)
    dy = dot_tn(spread, ditem_b)

    def back_hidden(rows, i):
        for c in range(0, FF, 256):
            h[rows, c : c + 256] = (
                u[rows, c : c + 256] * slope[rows, c : c + 256].astype(F32)
            ).astype(BF16)

    each(ROWS // 32, 32, back_hidden)
    ddown = dot_tn(hmean[...], ditem_b)
    for b in range(4):
        put_block(mlp_mine, b, ddown[b * W : (b + 1) * W])
    dup = dot_tn(n2[...], h[...])
    for b in range(4):
        put_block(mlp_mine, 4 + b, dup[:, b * W : (b + 1) * W])
    mlp_job.start()
    parent_job.scatter_first()
    u[:, :W] = dot_nt(h[...], up[...])
    u[:, W : 2 * W] = dy

    def back_stream(rows, i):
        x = s_[rows].astype(F32)
        r = rms_scale(x)
        unit = x * r
        dunit = u[rows, :W].astype(BF16).astype(F32) * hgain[...].astype(F32)
        dx = r * (dunit - unit * jnp.mean(dunit * unit, axis=1, keepdims=True))
        da[rows] = (dx + u[rows, W : 2 * W] * (1.0 / COLS)).astype(BF16)

    each(GROUPS, GROWS, back_stream, unroll=2)
    dmix[...] = dot_nt(da[...], co[...]).astype(BF16)
    put_block(att_mine, 3, dot_tn(mix[...], da[...]))
    mlp_job.scatter_first()
    parent_job.scatter_second()
    attend_back(q, k, v, probs, dmix, dqkv, GROUPS, GROWS)
    dweights = dot_tn(n1[...], dqkv[...])
    for b in range(3):
        put_block(att_mine, b, dweights[:, b * W : (b + 1) * W])
    att_job.start()

    mlp_job.scatter_second()
    att_job.scatter_first()
    parent_job.scatter_z()
    mlp_job.scatter_z()
    att_job.scatter_second()
    parent_job.gather_z()
    mlp_job.gather_z()
    att_job.scatter_z()
    parent_job.gather_second()
    mlp_job.gather_second()
    att_job.gather_z()
    parent_job.gather_first()
    mlp_job.gather_first()
    att_job.gather_second()
    parent_job.gather_core()
    mlp_job.gather_core()
    att_job.gather_first()
    att_job.gather_core()
    for job in (parent_job, mlp_job, att_job):
        job.finish()


def gain_row(weights, sums, gain):
    total = jnp.zeros((W, W), F32)
    for weight, value in zip(weights, sums, strict=True):
        total = total + weight.astype(F32) * value
    high = total.astype(BF16)
    low = (total - high.astype(F32)).astype(BF16)
    ones = jnp.ones((8, W), BF16)
    return (dot_nt(ones, high) + dot_nt(ones, low))[:1] / gain.astype(F32)


def unpack_kernel(
    states_in, parent_sum, mlp_sum, att_sum, cgain, cq, ck, cv, hgain, up, pgain, pq, pk, pv,
    states, dcg, dcq, dck, dcv, dco, dhg, dup, ddown, dlink, dpg, dpq, dpk, dpv, dpo,
):
    def block(total, b):
        return jnp.concatenate(
            [total[half, :, :, b].astype(F32).reshape(W, 128) for half in range(2)], axis=1
        )

    states[...] = states_in[...]
    grads = []
    for b, ref in enumerate((dcq, dck, dcv, dco)):
        grads.append(block(att_sum, b))
        ref[...] = grads[-1]
    dcg[...] = gain_row([cq[...], ck[...], cv[...]], grads[:3], cgain[...])
    grads = []
    for b in range(4):
        ddown[b * W : (b + 1) * W] = block(mlp_sum, b)
        grads.append(block(mlp_sum, 4 + b))
        dup[:, b * W : (b + 1) * W] = grads[-1]
    dhg[...] = gain_row([up[:, b * W : (b + 1) * W] for b in range(4)], grads, hgain[...])
    grads = []
    for b, ref in enumerate((dlink, dpq, dpk, dpv, dpo)):
        grads.append(block(parent_sum, b))
        ref[...] = grads[-1]
    dpg[...] = gain_row([pq[...], pk[...], pv[...]], grads[1:4], pgain[...])


def body(
    item_tokens, owner_index, owner_row, parent_tokens, cotangent,
    column_gain, column_query, column_key, column_value, column_out,
    hidden_gain, up_weight, down_weight, link_weight,
    parent_gain, parent_query, parent_key, parent_value, parent_out,
):
    vmem = pl.BlockSpec(memory_space=pltpu.VMEM)
    shape = jax.ShapeDtypeStruct
    cgain, hgain, pgain = (
        g.reshape(1, W) for g in (column_gain, hidden_gain, parent_gain)
    )
    items = lambda width, dtype=BF16: pltpu.VMEM((ROWS, width), dtype)
    parents = lambda width, dtype=BF16: pltpu.VMEM((PROWS, width), dtype)
    scratch = [
        items(W), items(W), items(W), items(W),
        pltpu.VMEM((GROUPS, HEADS * GROWS, GROWS), BF16),
        items(W), items(W), items(W), items(FF, F32), items(FF), items(FF),
        items(W), items(W), items(W), items(3 * W),
        pltpu.VMEM((TX, FF), BF16),
        parents(W), parents(W), parents(W), parents(W), parents(W),
        pltpu.VMEM((PGROUPS, HEADS * GPROWS, GPROWS), BF16),
        parents(W), parents(W), parents(W), parents(3 * W), parents(W, F32),
        pltpu.VMEM((2, 4, 4, 5, 16, 128), BF16),
        pltpu.VMEM((2, 4, 4, 8, 16, 128), BF16),
        pltpu.VMEM((2, 4, 4, 4, 16, 128), BF16),
        pltpu.VMEM((N_DP, 8, 128), F32),
        pltpu.VMEM((N_DP, 8, 128), F32),
        pltpu.VMEM((N_DP, 8, 128), F32),
        pltpu.VMEM((N_DP, 8, 128), F32),
        pltpu.SemaphoreType.DMA((2,)),
        pltpu.SemaphoreType.DMA((2,)),
    ]
    for n in (5, 8, 4):
        scratch += Summing.scratch(n)
    states, parent_sum, mlp_sum, att_sum = pl.pallas_call(
        encoder_kernel,
        out_shape=[shape((PROWS, W), BF16)]
        + [shape((2, 4, 4, n, 16, 128), BF16) for n in (5, 8, 4)],
        in_specs=[vmem] * 19,
        out_specs=[vmem] * 4,
        scratch_shapes=scratch,
        compiler_params=pltpu.CompilerParams(
            collective_id=1, has_side_effects=True, vmem_limit_bytes=VMEM_LIMIT
        ),
        name="encoder",
    )(
        item_tokens, owner_index.reshape(1, TX), owner_row.reshape(1, TX),
        parent_tokens.reshape(PROWS, W), cotangent.reshape(PROWS, W),
        cgain, column_query, column_key, column_value, column_out,
        hgain, up_weight, down_weight, link_weight,
        pgain, parent_query, parent_key, parent_value, parent_out,
    )
    square = shape((W, W), F32)
    row = shape((1, W), F32)
    out = pl.pallas_call(
        unpack_kernel,
        out_shape=[
            shape((PROWS, W), BF16), row, square, square, square, square, row,
            shape((W, FF), F32), shape((FF, W), F32), square, row, square, square, square, square,
        ],
        in_specs=[vmem] * 14,
        out_specs=[vmem] * 15,
        compiler_params=pltpu.CompilerParams(vmem_limit_bytes=VMEM_LIMIT),
        name="unpack",
    )(
        states, parent_sum, mlp_sum, att_sum, cgain, column_query, column_key, column_value,
        hgain, up_weight, pgain, parent_query, parent_key, parent_value,
    )
    out = [o.reshape(W) if o.shape == (1, W) else o for o in out]
    return (out[0].reshape(CUST, CTOK, W), *out[1:])


def solution(mesh):
    split, whole = P(("dp", "rep")), P()
    return jax.shard_map(
        body,
        mesh=mesh,
        in_specs=(split,) * 5 + (whole,) * 14,
        out_specs=(split,) + (whole,) * 14,
        check_vma=False,
    )
```

time: 299 us -> 100 us (0.33); the launches traced: 296 us -> 100 us
  blocking collectives: 74.8 us -> 0 us
  local copies, waits for them, and re-layouts: 63.9 us -> 2.55 us
  matrix products: 54.8 us -> 0 us
  other arithmetic: 14 us -> 0 us
  Pallas kernels: 86 us -> 96.8 us
    psum x1 -> x0, blocking collectives: 74.8 us -> none  [body(): gain_sums = list(lax.psum(jnp.stack(gains), ('dp', 'rep')))]
    dot_general x47 -> x0, matrix products: 50.9 us -> none  [the longest x32 30.7 us: project(): return jnp.einsum('...i,ij->...j', inputs.astype(jnp.float32), matrix)]
    reshape x17 -> x3, local copies, waits for them, and re-layouts: 24.5 us -> 1.74 us  [body(): g.reshape(1, W)]
    unnamed x211 -> x6, local copies, waits for them, and re-layouts: 14.8 us -> 0.8 us
    slice x7 -> x0, local copies, waits for them, and re-layouts: 13.7 us -> none  [the longest x5 13.7 us: body(): summed[offset:offset + gradient.size].reshape(gradient.shape)]
    pallas_call x3 -> x2, Pallas kernels: 86 us -> 96.8 us  [the longest x1 92.2 us: body(): pl.pallas_call(encoder_kernel, out_shape=[shape((PROWS, W), BF16)] + [sha...]
    convert_element_type x9 -> x0, local copies, waits for them, and re-layouts: 10.1 us -> none  [the longest x4 4.41 us: attention(): jnp.einsum('blhd,bmhd->bhlm', queries, key_rows, preferred_element_type=j...]
    sub x1 -> x0, other arithmetic: 7.05 us -> none  [attention(): weights = jax.nn.softmax(scores, axis=-1).astype(jnp.bfloat16)]
where the time goes in v2:
time: 100 us
  Pallas kernels  96.8 us (97%)
  local copies, waits for them, and re-layouts  2.55 us (3%)
    pallas_call x1, Pallas kernels, body(): pl.pallas_call(encoder_kernel, out_shape=[shape((PROWS, W), BF16)] + [sha...  92.2 us
    pallas_call x1, Pallas kernels, body(): pl.pallas_call(unpack_kernel, out_shape=[shape((PROWS, W), BF16), row, sq...  4.62 us

profile of v2, /device:TPU:1, one launch (start us, length us, event | category | flops | bytes accessed | tf_op | source)
XLA Modules:
  0.0 100.0 jit_solution(17267583671056770739)
XLA Ops:
  0.6 0.0 copy-start
  0.7 0.6 copy-done
  1.3 0.0 copy-start.1
  1.3 0.6 reshape.67.cgain
  1.9 0.1 copy-done.1
  2.0 0.0 copy-start.2
  2.0 0.6 reshape.68.hgain
  2.5 0.1 copy-done.2
  2.6 0.6 reshape.69.pgain
  3.2 92.2 %encoder.1 = (bf16[512,256]{1,0:T(8,128)(2,1)}, bf16[2,4,4,5,16,128]{5,4,3,2,1,0:T(8,128)(2,1)}, bf16[2,4,4,8,16,128]{5,4,3,2,1,0:T(8,128)(2,1)}, bf16[2,4,4,4,16,128]{5,4,3,2,1,0:T(8,128)(2,1)}) custom-call(bf16[24,24,256]{2,1,0:T(8,128)(2,1)} %item_ref.1, s32[1,24]{1,0:T(1,128)} %bitcast.10, s32[1,24]{1,0:T(1,128)} %bitcast.11, bf16[512,256]{1,0:T(8,128)(2,1)} %bitcast.8, ...), custom_call_target="tpu_custom_call" | custom-call | tf_op jit(solution)/shard_map/encoder/pallas_call | solution.py:634
  95.4 4.6 %unpack.1 = (bf16[512,256]{1,0:T(8,128)(2,1)}, f32[1,256]{1,0:T(1,128)}, f32[256,256]{1,0:T(8,128)}, f32[256,256]{1,0:T(8,128)}, f32[256,256]{1,0:T(8,128)}, /*i...) custom-call(bf16[512,256]{1,0:T(8,128)(2,1)} %get-tuple-element.34.s, ...), custom_call_target="tpu_custom_call" | custom-call | tf_op jit(solution)/shard_map/unpack/pallas_call | solution.py:654
Async XLA Ops:
  0.6 0.7 copy-start
  1.3 0.7 copy-start.1
  2.0 0.7 copy-start.2

commit v3 on v2

v3 whole, which is shorter than its diff:
```python
import math

import jax
import jax.numpy as jnp
from jax import lax
from jax.experimental import pallas as pl
from jax.experimental.pallas import tpu as pltpu
from jax.sharding import PartitionSpec as P

MESH = pl.DeviceIdType.MESH
F32 = jnp.float32
BF16 = jnp.bfloat16
N_DP = 64


def place():
    dp, rep = lax.axis_index("dp"), lax.axis_index("rep")
    z, x, core = lax.div(dp, 8), lax.rem(lax.div(dp, 2), 4), lax.rem(dp, 2)
    return dp, rep, z, core, rep * 4 + x


def core_peer(at):
    dp, rep, z, core, spot = at
    return (dp + 1 - 2 * core, rep)


def plane_peer(at, j):
    dp, rep, z, core, spot = at
    return (8 * z + 2 * lax.rem(j, 4) + core, lax.div(j, 4))


def z_peer(at, j):
    dp, rep, z, core, spot = at
    return (8 * j + lax.rem(dp, 8), rep)


def remote(src, dst, send, recv, peer):
    copy = pltpu.make_async_remote_copy(
        src_ref=src, dst_ref=dst, send_sem=send, recv_sem=recv, device_id=peer, device_id_type=MESH
    )
    copy.start()
    return copy


def wait_sent(at, like, sem):
    pltpu.make_async_remote_copy(
        src_ref=like, dst_ref=like, send_sem=sem, recv_sem=sem,
        device_id=core_peer(at), device_id_type=MESH,
    ).wait_send()


def wait_received(at, like, sem):
    pltpu.make_async_remote_copy(
        src_ref=like, dst_ref=like, send_sem=sem, recv_sem=sem,
        device_id=core_peer(at), device_id_type=MESH,
    ).wait_recv()


class Summing:
    def __init__(self, at, n, mine, total, scratch):
        self.at, self.n, self.mine, self.total = at, n, mine, total
        self.core_in, self.plane_out, self.plane_in, self.z_all, self.send, self.recv = scratch

    @staticmethod
    def scratch(n):
        return [
            pltpu.VMEM((16, n, 16, 128), BF16),
            pltpu.VMEM((16, n, 16, 128), BF16),
            pltpu.VMEM((15, n, 16, 128), BF16),
            pltpu.VMEM((8, n, 16, 128), BF16),
            pltpu.SemaphoreType.DMA((5,)),
            pltpu.SemaphoreType.DMA((20,)),
        ]

    def start(self):
        dp, rep, z, core, spot = self.at
        self.from_core = remote(
            self.mine.at[1 - core], self.core_in, self.send.at[0], self.recv.at[0], core_peer(self.at)
        )

    def scatter_plane(self):
        dp, rep, z, core, spot = self.at
        self.from_core.wait_recv()
        self.plane_out[...] = (
            self.mine[core].astype(F32) + self.core_in[...].astype(F32)
        ).astype(BF16)
        for d in range(1, 16):
            q = lax.rem(spot + d, 16)
            remote(
                self.plane_out.at[q], self.plane_in.at[d - 1], self.send.at[1], self.recv.at[1],
                plane_peer(self.at, q),
            )

    def scatter_z(self):
        dp, rep, z, core, spot = self.at
        wait_received(self.at, self.plane_in, self.recv.at[1])
        value = self.plane_out[spot].astype(F32)
        for i in range(15):
            value = value + self.plane_in[i].astype(F32)
        self.z_all[z] = value.astype(BF16)
        for d in range(1, 8):
            here = self.z_all.at[z]
            remote(here, here, self.send.at[2], self.recv.at[2], z_peer(self.at, lax.rem(z + d, 8)))

    def gather_plane(self):
        dp, rep, z, core, spot = self.at
        wait_received(self.at, self.z_all.at[pl.ds(0, 7)], self.recv.at[2])
        value = self.z_all[0].astype(F32)
        for i in range(1, 8):
            value = value + self.z_all[i].astype(F32)
        self.total[core, spot] = value.astype(BF16)
        here = self.total.at[core, spot]
        self.from_plane = [
            remote(
                here, here, self.send.at[3], self.recv.at[3 + d],
                plane_peer(self.at, lax.rem(spot + d, 16)),
            )
            for d in range(1, 16)
        ]
        remote(here, here, self.send.at[4], self.recv.at[3], core_peer(self.at))

    def gather_core(self):
        dp, rep, z, core, spot = self.at
        for d, copy in zip(range(1, 16), self.from_plane, strict=True):
            copy.wait_recv()
            here = self.total.at[core, lax.rem(spot + 16 - d, 16)]
            remote(here, here, self.send.at[4], self.recv.at[3], core_peer(self.at))

    def finish(self):
        dp, rep, z, core, spot = self.at
        wait_received(self.at, self.total.at[1 - core], self.recv.at[3])
        self.from_core.wait_send()
        wait_sent(self.at, self.plane_in, self.send.at[1])
        wait_sent(self.at, self.z_all.at[pl.ds(0, 7)], self.send.at[2])
        wait_sent(self.at, self.total.at[core, pl.ds(0, 15)], self.send.at[3])
        wait_sent(self.at, self.total.at[core], self.send.at[4])


def exchange_start(at, out_ref, in_ref, send, recv):
    dp, rep = at[:2]
    in_ref[dp] = out_ref[dp]

    def to(d):
        j = lax.rem(dp + d, N_DP)
        remote(out_ref.at[j], in_ref.at[dp], send, recv, (j, rep))

    def step(d, carry):
        to(N_DP // 2 - d)
        to(N_DP // 2 + d)
        return carry

    to(N_DP // 2)
    lax.fori_loop(1, N_DP // 2, step, 0)


def exchange_wait(at, in_ref, send, recv):
    rest = in_ref.at[pl.ds(0, N_DP - 1)]
    wait_received(at, rest, recv)
    wait_sent(at, rest, send)


def greet_all(at, barrier):
    dp, rep, z, core, spot = at

    def group(d, carry):
        peer = (lax.rem(dp + d, N_DP), rep)
        pl.semaphore_signal(barrier, inc=1, device_id=peer, device_id_type=MESH)
        return carry

    lax.fori_loop(1, N_DP, group, 0)
    for d in range(1, 4):
        for x in range(4):
            peer = (8 * z + 2 * x + core, lax.rem(rep + d, 4))
            pl.semaphore_signal(barrier, inc=1, device_id=peer, device_id_type=MESH)
    return N_DP - 1 + 12


VMEM_LIMIT = 56 * 1024 * 1024
EPSILON = 1e-06
HEADS = 8
W = 256
HEAD = 32
FF = 1024
TX, COLS = 24, 24
CUST, CTOK = 16, 32
ROWS = TX * COLS
PROWS = CUST * CTOK
GROUP = 4
GROWS = GROUP * COLS
GPROWS = GROUP * CTOK
GROUPS = TX // GROUP
PGROUPS = CUST // GROUP


def dot(a, b):
    return lax.dot_general(a, b, (((1,), (0,)), ((), ())), preferred_element_type=F32)


def dot_nt(a, b):
    return lax.dot_general(a, b, (((1,), (1,)), ((), ())), preferred_element_type=F32)


def dot_tn(a, b):
    return lax.dot_general(a, b, (((0,), (0,)), ((), ())), preferred_element_type=F32)


def each(count, step, body, unroll=1):
    def one(i, carry):
        body(pl.ds(pl.multiple_of(i * step, step), step), i)
        return carry

    lax.fori_loop(0, count, one, 0, unroll=unroll)


def head_masks():
    lane = lax.broadcasted_iota(jnp.int32, (1, W), 1)
    return [jnp.where(lax.div(lane, HEAD) == h, 1.0, 0.0) for h in range(HEADS)]


def spread_heads(value, masks):
    return jnp.concatenate([value * mask.astype(BF16) for mask in masks], axis=0)


def join_heads(value, masks, rows):
    total = value[:rows] * masks[0]
    for h in range(1, HEADS):
        total = total + value[h * rows : (h + 1) * rows] * masks[h]
    return total


def same_owner(rows, length):
    i = lax.div(lax.broadcasted_iota(jnp.int32, (rows, rows), 0), length)
    j = lax.div(lax.broadcasted_iota(jnp.int32, (rows, rows), 1), length)
    return jnp.concatenate([jnp.where(i == j, 0.0, -1e30)] * HEADS, axis=0)


def attend(q, k, v, probs, mix, groups, rows, length):
    masks = head_masks()
    bias = same_owner(rows, length)

    def body(at, i):
        wide = spread_heads(q[at], masks)
        scores = dot_nt(wide, k[at]) * HEAD**-0.5 + bias
        e = jnp.exp(scores - jnp.max(scores, axis=1, keepdims=True))
        p = (e * (1.0 / jnp.sum(e, axis=1, keepdims=True))).astype(BF16)
        probs[i] = p
        mix[at] = join_heads(dot(p, v[at]), masks, rows).astype(BF16)

    each(groups, rows, body)


def attend_back(q, k, v, probs, dmix, dqkv, groups, rows):
    masks = head_masks()

    def body(at, i):
        p = probs[i]
        wide_d = spread_heads(dmix[at], masks)
        wide_q = spread_heads(q[at], masks)
        dp = dot_nt(wide_d, v[at]).astype(BF16).astype(F32)
        weighted = p.astype(F32)
        ds = weighted * (dp - jnp.sum(weighted * dp, axis=1, keepdims=True))
        ds = (ds * HEAD**-0.5).astype(BF16)
        dqkv[at, 0:W] = join_heads(dot(ds, k[at]), masks, rows).astype(BF16)
        dqkv[at, W : 2 * W] = dot_tn(ds, wide_q).astype(BF16)
        dqkv[at, 2 * W : 3 * W] = dot_tn(p, wide_d).astype(BF16)

    each(groups, rows, body)


def put_block(mine, b, value):
    for half in range(2):
        part = value[:, half * 128 : (half + 1) * 128].astype(BF16)
        mine[half, :, b] = part.reshape(16, 16, 128)


def rms_scale(value):
    return lax.rsqrt(jnp.mean(value * value, axis=1, keepdims=True) + EPSILON)


def averaging():
    t = lax.broadcasted_iota(jnp.int32, (TX, ROWS), 0)
    r = lax.div(lax.broadcasted_iota(jnp.int32, (TX, ROWS), 1), COLS)
    return jnp.where(t == r, 1.0, 0.0).astype(BF16)


def placing(owner_ref):
    owner = owner_ref[...]
    i = lax.broadcasted_iota(jnp.int32, (TX, TX), 0)
    j = lax.broadcasted_iota(jnp.int32, (TX, TX), 1)
    along = jnp.broadcast_to(owner, (TX, TX))
    down = jnp.sum(jnp.where(i == j, along, 0), axis=1, keepdims=True)
    slot = jnp.sum(jnp.where((down == along) & (i < j), 1, 0), axis=0, keepdims=True)
    device = lax.broadcasted_iota(jnp.int32, (N_DP, TX), 0)
    goes = device == jnp.broadcast_to(owner, (N_DP, TX))
    return [
        jnp.where(goes & (jnp.broadcast_to(slot, (N_DP, TX)) == s), 1.0, 0.0).astype(BF16)
        for s in range(2)
    ]


def encoder_kernel(
    item_ref, owner_ref, row_ref, parent_ref, cot_ref,
    cgain, cq, ck, cv, co, hgain, up, down, link, pgain, pq, pk, pv, po,
    states_ref, parent_sum, down_sum, up_sum, att_sum,
    n1, q, k, v, probs, mix, s_, n2, u, h, slope, dn2, da, dmix, dqkv, hmean,
    pbased, pn, pq_, pk_, pv_, pprobs, pmix, pda, pdmix, pdqkv, pdn,
    parent_mine, down_mine, up_mine, att_mine,
    out1, in1, out2, in2, x_send, x_recv,
    *job_scratch,
):
    at = place()
    barrier = pltpu.get_barrier_semaphore()
    greeted = greet_all(at, barrier)
    jobs = zip(
        (5, 4, 4, 4),
        (parent_mine, down_mine, up_mine, att_mine),
        (parent_sum, down_sum, up_sum, att_sum),
        strict=True,
    )
    per = len(job_scratch) // 4
    parent_job, down_job, up_job, att_job = [
        Summing(at, *job, job_scratch[i * per : (i + 1) * per]) for i, job in enumerate(jobs)
    ]

    def norm_items(rows, i):
        x = item_ref[pl.ds(i * GROUP, GROUP)].astype(F32).reshape(GROWS, W)
        n1[rows] = (x * rms_scale(x) * cgain[...].astype(F32)[None, :]).astype(BF16)

    each(GROUPS, GROWS, norm_items, unroll=2)
    q[...] = dot(n1[...], cq[...]).astype(BF16)
    k[...] = dot(n1[...], ck[...]).astype(BF16)
    v[...] = dot(n1[...], cv[...]).astype(BF16)
    attend(q, k, v, probs, mix, GROUPS, GROWS, COLS)
    u[:, :W] = dot(mix[...], co[...])

    def norm_stream(rows, i):
        x = item_ref[pl.ds(i * GROUP, GROUP)].astype(F32).reshape(GROWS, W)
        stream = (x + u[rows, :W]).astype(BF16)
        s_[rows] = stream
        stream = stream.astype(F32)
        n2[rows] = (stream * rms_scale(stream) * hgain[...].astype(F32)[None, :]).astype(BF16)

    each(GROUPS, GROWS, norm_stream, unroll=2)
    u[...] = dot(n2[...], up[...])

    def gelu(rows, i):
        for c in range(0, FF, 256):
            value = u[rows, c : c + 256]
            square = value * value
            t = jnp.tanh(math.sqrt(2.0 / math.pi) * value * (1.0 + 0.044715 * square))
            half = 0.5 * (1.0 + t)
            h[rows, c : c + 256] = (value * half).astype(BF16)
            inner = math.sqrt(2.0 / math.pi) * (1.0 + 3 * 0.044715 * square)
            slope[rows, c : c + 256] = (half + 0.5 * value * (1.0 - t * t) * inner).astype(BF16)

    each(ROWS // 32, 32, gelu)
    average = averaging()
    hidden = (dot(average, h[...]) * (1.0 / COLS)).astype(BF16)
    hmean[...] = hidden
    embedding = (dot(average, s_[...]) * (1.0 / COLS) + dot(hidden, down[...])).astype(BF16)

    places = placing(owner_ref)
    ids = jnp.broadcast_to(row_ref[...].astype(F32) + 1.0, (128, TX)).astype(BF16)
    for slot in range(2):
        moved = dot(places[slot], embedding)
        out1[:, 2 * slot, :] = moved[:, :128]
        out1[:, 2 * slot + 1, :] = moved[:, 128:]
        out1[:, 4 + slot, :] = dot_nt(places[slot], ids)
        out1[:, 6 + slot, :] = jnp.zeros((N_DP, 128), F32)
    pl.semaphore_wait(barrier, greeted)
    exchange_start(at, out1, in1, x_send.at[0], x_recv.at[0])
    exchange_wait(at, in1, x_send.at[0], x_recv.at[0])

    members = []
    customer = lax.broadcasted_iota(jnp.int32, (N_DP, CUST), 1).astype(F32) + 1.0
    counts, sums = jnp.zeros((CUST, W), F32), jnp.zeros((CUST, W), F32)
    for slot in range(2):
        got = jnp.concatenate([in1[:, 2 * slot, :], in1[:, 2 * slot + 1, :]], axis=1).astype(BF16)
        member = jnp.where(in1[:, 4 + slot, :][:, :CUST] == customer, 1.0, 0.0).astype(BF16)
        members.append(member)
        counts = counts + dot_tn(member, jnp.ones((N_DP, W), BF16))
        sums = sums + dot_tn(member, got)
    divisor = jnp.maximum(counts, 1.0)
    pooled = (sums / divisor).astype(BF16)
    linked = dot(pooled, link[...])
    scale = 1.0 / math.sqrt(CUST * CTOK * 256)
    pbased_value = (
        (parent_ref[...].astype(F32).reshape(CUST, CTOK, W) + linked[:, None, :])
        .astype(BF16)
        .reshape(PROWS, W)
    )
    pbased[...] = pbased_value

    def norm_based(rows, i):
        x = pbased[rows].astype(F32)
        pn[rows] = (x * rms_scale(x) * pgain[...].astype(F32)[None, :]).astype(BF16)
        pda[rows] = (cot_ref[rows].astype(F32) * scale).astype(BF16)

    each(PGROUPS, GPROWS, norm_based, unroll=2)
    pq_[...] = dot(pn[...], pq[...]).astype(BF16)
    pk_[...] = dot(pn[...], pk[...]).astype(BF16)
    pv_[...] = dot(pn[...], pv[...]).astype(BF16)
    pdmix[...] = dot_nt(pda[...], po[...]).astype(BF16)
    attend(pq_, pk_, pv_, pprobs, pmix, PGROUPS, GPROWS, CTOK)
    attend_back(pq_, pk_, pv_, pprobs, pdmix, pdqkv, PGROUPS, GPROWS)
    pdn[...] = (
        dot_nt(pdqkv[:, :W], pq[...])
        + dot_nt(pdqkv[:, W : 2 * W], pk[...])
        + dot_nt(pdqkv[:, 2 * W :], pv[...])
    )

    dlinked = []
    for i in range(PGROUPS):
        rows = slice(i * GPROWS, (i + 1) * GPROWS)
        x = pbased[rows].astype(F32)
        r = rms_scale(x)
        unit = x * r
        dunit = pdn[rows] * pgain[...].astype(F32)[None, :]
        dx = r * (dunit - unit * jnp.mean(dunit * unit, axis=1, keepdims=True))
        dx = dx + cot_ref[rows].astype(F32) * scale
        dlinked.append(jnp.sum(dx.reshape(GROUP, CTOK, W), axis=1))
    dlinked = jnp.concatenate(dlinked, axis=0)
    dpooled = dot_nt(dlinked.astype(BF16), link[...]).astype(BF16).astype(F32)
    sum_grad = (dpooled / divisor).astype(BF16)
    for slot in range(2):
        moved = dot(members[slot], sum_grad)
        out2[:, 2 * slot, :] = moved[:, :128]
        out2[:, 2 * slot + 1, :] = moved[:, 128:]
        out2[:, 4 + slot, :] = jnp.zeros((N_DP, 128), F32)
        out2[:, 6 + slot, :] = jnp.zeros((N_DP, 128), F32)
    exchange_start(at, out2, in2, x_send.at[1], x_recv.at[1])

    put_block(parent_mine, 0, dot_tn(pooled, dlinked.astype(BF16)))
    dweights = dot_tn(pn[...], pdqkv[...])
    for b in range(3):
        put_block(parent_mine, 1 + b, dweights[:, b * W : (b + 1) * W])
    put_block(parent_mine, 4, dot_tn(pmix[...], pda[...]))
    parent_job.start()
    states_ref[...] = (pbased[...].astype(F32) + dot(pmix[...], po[...])).astype(BF16)
    parent_job.scatter_plane()
    exchange_wait(at, in2, x_send.at[1], x_recv.at[1])

    ditem = jnp.zeros((TX, W), F32)
    for slot in range(2):
        got = jnp.concatenate([in2[:, 2 * slot, :], in2[:, 2 * slot + 1, :]], axis=1).astype(BF16)
        ditem = ditem + dot_tn(places[slot], got)
    ditem_b = ditem.astype(BF16)
    ddown = dot_tn(hmean[...], ditem_b)
    for b in range(4):
        put_block(down_mine, b, ddown[b * W : (b + 1) * W])
    down_job.start()
    dhidden = (dot_nt(ditem_b, down[...]) * (1.0 / COLS)).astype(BF16)
    spread = averaging()
    u[...] = dot_tn(spread, dhidden)
    dy = dot_tn(spread, ditem_b)

    def back_hidden(rows, i):
        for c in range(0, FF, 256):
            h[rows, c : c + 256] = (
                u[rows, c : c + 256] * slope[rows, c : c + 256].astype(F32)
            ).astype(BF16)

    each(ROWS // 32, 32, back_hidden)
    down_job.scatter_plane()
    dup = dot_tn(n2[...], h[...])
    for b in range(4):
        put_block(up_mine, b, dup[:, b * W : (b + 1) * W])
    up_job.start()
    parent_job.scatter_z()
    u[:, :W] = dot_nt(h[...], up[...])
    u[:, W : 2 * W] = dy

    def back_stream(rows, i):
        x = s_[rows].astype(F32)
        r = rms_scale(x)
        unit = x * r
        dunit = u[rows, :W].astype(BF16).astype(F32) * hgain[...].astype(F32)[None, :]
        dx = r * (dunit - unit * jnp.mean(dunit * unit, axis=1, keepdims=True))
        da[rows] = (dx + u[rows, W : 2 * W] * (1.0 / COLS)).astype(BF16)

    each(GROUPS, GROWS, back_stream, unroll=2)
    up_job.scatter_plane()
    dmix[...] = dot_nt(da[...], co[...]).astype(BF16)
    put_block(att_mine, 3, dot_tn(mix[...], da[...]))
    attend_back(q, k, v, probs, dmix, dqkv, GROUPS, GROWS)
    dweights = dot_tn(n1[...], dqkv[...])
    for b in range(3):
        put_block(att_mine, b, dweights[:, b * W : (b + 1) * W])
    att_job.start()

    parent_job.gather_plane()
    down_job.scatter_z()
    att_job.scatter_plane()
    up_job.scatter_z()
    parent_job.gather_core()
    down_job.gather_plane()
    att_job.scatter_z()
    up_job.gather_plane()
    down_job.gather_core()
    att_job.gather_plane()
    up_job.gather_core()
    att_job.gather_core()
    for job in (parent_job, down_job, up_job, att_job):
        job.finish()


def gain_row(weights, sums, gain):
    total = jnp.zeros((W, W), F32)
    for weight, value in zip(weights, sums, strict=True):
        total = total + weight.astype(F32) * value
    high = total.astype(BF16)
    low = (total - high.astype(F32)).astype(BF16)
    ones = jnp.ones((8, W), BF16)
    return (dot_nt(ones, high) + dot_nt(ones, low))[:1] / gain.astype(F32)[None, :]


def unpack_kernel(
    states_in, parent_sum, down_sum, up_sum, att_sum, cgain, cq, ck, cv, hgain, up, pgain, pq, pk, pv,
    states, dcg, dcq, dck, dcv, dco, dhg, dup, ddown, dlink, dpg, dpq, dpk, dpv, dpo,
):
    def block(total, b):
        return jnp.concatenate(
            [total[half, :, b].astype(F32).reshape(W, 128) for half in range(2)], axis=1
        )

    states[...] = states_in[...]
    grads = []
    for b, ref in enumerate((dcq, dck, dcv, dco)):
        grads.append(block(att_sum, b))
        ref[...] = grads[-1]
    dcg[...] = gain_row([cq[...], ck[...], cv[...]], grads[:3], cgain[...])
    grads = []
    for b in range(4):
        ddown[b * W : (b + 1) * W] = block(down_sum, b)
        grads.append(block(up_sum, b))
        dup[:, b * W : (b + 1) * W] = grads[-1]
    dhg[...] = gain_row([up[:, b * W : (b + 1) * W] for b in range(4)], grads, hgain[...])
    grads = []
    for b, ref in enumerate((dlink, dpq, dpk, dpv, dpo)):
        grads.append(block(parent_sum, b))
        ref[...] = grads[-1]
    dpg[...] = gain_row([pq[...], pk[...], pv[...]], grads[1:4], pgain[...])


def body(
    item_tokens, owner_index, owner_row, parent_tokens, cotangent,
    column_gain, column_query, column_key, column_value, column_out,
    hidden_gain, up_weight, down_weight, link_weight,
    parent_gain, parent_query, parent_key, parent_value, parent_out,
):
    vmem = pl.BlockSpec(memory_space=pltpu.VMEM)
    shape = jax.ShapeDtypeStruct
    cgain, hgain, pgain = column_gain, hidden_gain, parent_gain
    items = lambda width, dtype=BF16: pltpu.VMEM((ROWS, width), dtype)
    parents = lambda width, dtype=BF16: pltpu.VMEM((PROWS, width), dtype)
    scratch = [
        items(W), items(W), items(W), items(W),
        pltpu.VMEM((GROUPS, HEADS * GROWS, GROWS), BF16),
        items(W), items(W), items(W), items(FF, F32), items(FF), items(FF),
        items(W), items(W), items(W), items(3 * W),
        pltpu.VMEM((TX, FF), BF16),
        parents(W), parents(W), parents(W), parents(W), parents(W),
        pltpu.VMEM((PGROUPS, HEADS * GPROWS, GPROWS), BF16),
        parents(W), parents(W), parents(W), parents(3 * W), parents(W, F32),
        *[pltpu.VMEM((2, 16, n, 16, 128), BF16) for n in (5, 4, 4, 4)],
        pltpu.VMEM((N_DP, 8, 128), F32),
        pltpu.VMEM((N_DP, 8, 128), F32),
        pltpu.VMEM((N_DP, 8, 128), F32),
        pltpu.VMEM((N_DP, 8, 128), F32),
        pltpu.SemaphoreType.DMA((2,)),
        pltpu.SemaphoreType.DMA((2,)),
    ]
    for n in (5, 4, 4, 4):
        scratch += Summing.scratch(n)
    states, parent_sum, down_sum, up_sum, att_sum = pl.pallas_call(
        encoder_kernel,
        out_shape=[shape((PROWS, W), BF16)]
        + [shape((2, 16, n, 16, 128), BF16) for n in (5, 4, 4, 4)],
        in_specs=[vmem] * 19,
        out_specs=[vmem] * 5,
        scratch_shapes=scratch,
        compiler_params=pltpu.CompilerParams(
            collective_id=1, has_side_effects=True, vmem_limit_bytes=VMEM_LIMIT
        ),
        name="encoder",
    )(
        item_tokens, owner_index.reshape(1, TX), owner_row.reshape(1, TX),
        parent_tokens.reshape(PROWS, W), cotangent.reshape(PROWS, W),
        cgain, column_query, column_key, column_value, column_out,
        hgain, up_weight, down_weight, link_weight,
        pgain, parent_query, parent_key, parent_value, parent_out,
    )
    square = shape((W, W), F32)
    row = shape((1, W), F32)
    out = pl.pallas_call(
        unpack_kernel,
        out_shape=[
            shape((PROWS, W), BF16), row, square, square, square, square, row,
            shape((W, FF), F32), shape((FF, W), F32), square, row, square, square, square, square,
        ],
        in_specs=[vmem] * 15,
        out_specs=[vmem] * 15,
        compiler_params=pltpu.CompilerParams(vmem_limit_bytes=VMEM_LIMIT),
        name="unpack",
    )(
        states, parent_sum, down_sum, up_sum, att_sum, cgain, column_query, column_key, column_value,
        hgain, up_weight, pgain, parent_query, parent_key, parent_value,
    )
    out = [o.reshape(W) if o.shape == (1, W) else o for o in out]
    return (out[0].reshape(CUST, CTOK, W), *out[1:])


def solution(mesh):
    split, whole = P(("dp", "rep")), P()
    return jax.shard_map(
        body,
        mesh=mesh,
        in_specs=(split,) * 5 + (whole,) * 14,
        out_specs=(split,) + (whole,) * 14,
        check_vma=False,
    )
```

time: 100 us -> 86.7 us (0.87)
  Pallas kernels: 96.8 us -> 85.9 us
  local copies, waits for them, and re-layouts: 2.55 us -> 0 us
    pallas_call x1, Pallas kernels: 92.2 us -> 81.4 us  [body(): pl.pallas_call(encoder_kernel, out_shape=[shape((PROWS, W), BF16)] + [sha...]
    reshape x3 -> x0, local copies, waits for them, and re-layouts: 1.74 us -> none  [body(): g.reshape(1, W)]
where the time goes in v3:
time: 86.7 us; the launch traced here: 86.5 us
  Pallas kernels  85.9 us (99%)
    pallas_call x1, Pallas kernels, body(): pl.pallas_call(encoder_kernel, out_shape=[shape((PROWS, W), BF16)] + [sha...  81.4 us
    pallas_call x1, Pallas kernels, body(): pl.pallas_call(unpack_kernel, out_shape=[shape((PROWS, W), BF16), row, sq...  4.52 us

profile of v3, /device:TPU:1, one launch (start us, length us, event | category | flops | bytes accessed | tf_op | source)
XLA Modules:
  0.0 86.5 jit_solution(6717727804413462156)
XLA Ops:
  0.6 81.4 %encoder.1 = (bf16[512,256]{1,0:T(8,128)(2,1)}, bf16[2,16,5,16,128]{4,3,2,1,0:T(8,128)(2,1)}, bf16[2,16,4,16,128]{4,3,2,1,0:T(8,128)(2,1)}, bf16[2,16,4,16,128]{...) custom-call(bf16[24,24,256]{2,1,0:T(8,128)(2,1)} %item_ref.1, s32[1,24]{1,0:T(1,128)} %bitcast.10, s32[1,24]{1,0:T(1,128)} %bitcast.11, ...), custom_call_target="tpu_custom_call" | custom-call | tf_op jit(solution)/shard_map/encoder/pallas_call | solution.py:575
  82.0 4.5 %unpack.1 = (bf16[512,256]{1,0:T(8,128)(2,1)}, f32[1,256]{1,0:T(1,128)}, f32[256,256]{1,0:T(8,128)}, f32[256,256]{1,0:T(8,128)}, f32[256,256]{1,0:T(8,128)}, /*i...) custom-call(bf16[512,256]{1,0:T(8,128)(2,1)} %get-tuple-element.35.s, ...), custom_call_target="tpu_custom_call" | custom-call | tf_op jit(solution)/shard_map/unpack/pallas_call | solution.py:595

commit v4 on v3

--- a/solution.py
+++ b/solution.py
@@ -10,7 +10,7 @@
 MESH = pl.DeviceIdType.MESH
 F32 = jnp.float32
 BF16 = jnp.bfloat16
-N_DP = 64
+CHIPS = 32
 
 
 def place():
@@ -136,47 +136,84 @@
         wait_sent(self.at, self.total.at[core], self.send.at[4])
 
 
-def exchange_start(at, out_ref, in_ref, send, recv):
-    dp, rep = at[:2]
-    in_ref[dp] = out_ref[dp]
-
-    def to(d):
-        j = lax.rem(dp + d, N_DP)
-        remote(out_ref.at[j], in_ref.at[dp], send, recv, (j, rep))
-
-    def step(d, carry):
-        to(N_DP // 2 - d)
-        to(N_DP // 2 + d)
-        return carry
-
-    to(N_DP // 2)
-    lax.fori_loop(1, N_DP // 2, step, 0)
-
-
-def exchange_wait(at, in_ref, send, recv):
-    rest = in_ref.at[pl.ds(0, N_DP - 1)]
-    wait_received(at, rest, recv)
-    wait_sent(at, rest, send)
+class Exchange:
+    def __init__(self, at, scratch):
+        self.at = at
+        self.wide, self.out, self.near, self.far, self.send, self.recv = scratch
+
+    @staticmethod
+    def scratch():
+        return [
+            pltpu.VMEM((CHIPS, 16, 128), F32),
+            pltpu.VMEM((CHIPS, 16, 128), BF16),
+            pltpu.VMEM((CHIPS, 16, 128), BF16),
+            pltpu.VMEM((CHIPS, 16, 128), BF16),
+            pltpu.SemaphoreType.DMA((2,)),
+            pltpu.SemaphoreType.DMA((2,)),
+        ]
+
+    def put(self, p, value, extra=None):
+        self.wide[:, 2 * p, :] = value[:, :128]
+        self.wide[:, 2 * p + 1, :] = value[:, 128:]
+        self.wide[:, 8 + p, :] = jnp.zeros((CHIPS, 128), F32) if extra is None else extra
+        self.wide[:, 12 + p, :] = jnp.zeros((CHIPS, 128), F32)
+
+    def start(self):
+        dp, rep, z, core, spot = self.at
+        chip = lax.div(dp, 2)
+        self.out[...] = self.wide[...].astype(BF16)
+        self.near[chip] = self.out[chip]
+
+        def to(d):
+            j = lax.rem(chip + d, CHIPS)
+            remote(
+                self.out.at[j], self.near.at[chip], self.send.at[0], self.recv.at[0],
+                (2 * j + core, rep),
+            )
+
+        to(CHIPS // 2)
+        for d in range(1, CHIPS // 2):
+            to(CHIPS // 2 - d)
+            to(CHIPS // 2 + d)
+
+    def wait(self):
+        rest = self.near.at[pl.ds(0, CHIPS - 1)]
+        wait_received(self.at, rest, self.recv.at[0])
+        across = remote(
+            self.near, self.far, self.send.at[1], self.recv.at[1], core_peer(self.at)
+        )
+        wait_sent(self.at, rest, self.send.at[0])
+        across.wait_recv()
+        across.wait_send()
+
+    def rows(self, source):
+        dp, rep, z, core, spot = self.at
+        wide = self.wide
+        wide[...] = source[...].astype(F32)
+        mine = lambda r, step: jnp.where(core == 0, wide[:, r, :], wide[:, r + step, :])
+        return [
+            (
+                jnp.concatenate([mine(2 * slot, 4), mine(2 * slot + 1, 4)], axis=1).astype(BF16),
+                mine(8 + slot, 2),
+            )
+            for slot in range(2)
+        ]
 
 
 def greet_all(at, barrier):
     dp, rep, z, core, spot = at
-
-    def group(d, carry):
-        peer = (lax.rem(dp + d, N_DP), rep)
+    chip = lax.div(dp, 2)
+    peers = [(2 * lax.rem(chip + d, CHIPS) + core, rep) for d in range(1, CHIPS)]
+    peers += [core_peer(at)]
+    peers += [(8 * z + 2 * x + core, lax.rem(rep + d, 4)) for d in range(1, 4) for x in range(4)]
+    for peer in peers:
         pl.semaphore_signal(barrier, inc=1, device_id=peer, device_id_type=MESH)
-        return carry
-
-    lax.fori_loop(1, N_DP, group, 0)
-    for d in range(1, 4):
-        for x in range(4):
-            peer = (8 * z + 2 * x + core, lax.rem(rep + d, 4))
-            pl.semaphore_signal(barrier, inc=1, device_id=peer, device_id_type=MESH)
-    return N_DP - 1 + 12
+    return len(peers)
 
 
 VMEM_LIMIT = 56 * 1024 * 1024
 EPSILON = 1e-06
+ROOT = math.sqrt(2.0 / math.pi)
 HEADS = 8
 W = 256
 HEAD = 32
@@ -237,8 +274,8 @@
 def attend(q, k, v, probs, mix, groups, rows, length):
     masks = head_masks()
     bias = same_owner(rows, length)
-
-    def body(at, i):
+    for i in range(groups):
+        at = slice(i * rows, (i + 1) * rows)
         wide = spread_heads(q[at], masks)
         scores = dot_nt(wide, k[at]) * HEAD**-0.5 + bias
         e = jnp.exp(scores - jnp.max(scores, axis=1, keepdims=True))
@@ -246,25 +283,23 @@
         probs[i] = p
         mix[at] = join_heads(dot(p, v[at]), masks, rows).astype(BF16)
 
-    each(groups, rows, body)
-
-
-def attend_back(q, k, v, probs, dmix, dqkv, groups, rows):
+
+def attend_back(q, k, v, probs, dmix, dqkv, groups, rows, meanwhile=None):
     masks = head_masks()
-
-    def body(at, i):
+    for i in range(groups):
+        at = slice(i * rows, (i + 1) * rows)
         p = probs[i]
         wide_d = spread_heads(dmix[at], masks)
         wide_q = spread_heads(q[at], masks)
-        dp = dot_nt(wide_d, v[at]).astype(BF16).astype(F32)
         weighted = p.astype(F32)
-        ds = weighted * (dp - jnp.sum(weighted * dp, axis=1, keepdims=True))
+        ds = weighted * dot_nt(wide_d, v[at])
+        ds = ds - weighted * jnp.sum(ds, axis=1, keepdims=True)
         ds = (ds * HEAD**-0.5).astype(BF16)
         dqkv[at, 0:W] = join_heads(dot(ds, k[at]), masks, rows).astype(BF16)
         dqkv[at, W : 2 * W] = dot_tn(ds, wide_q).astype(BF16)
         dqkv[at, 2 * W : 3 * W] = dot_tn(p, wide_d).astype(BF16)
-
-    each(groups, rows, body)
+        if meanwhile is not None:
+            meanwhile(i)
 
 
 def put_block(mine, b, value):
@@ -290,24 +325,41 @@
     along = jnp.broadcast_to(owner, (TX, TX))
     down = jnp.sum(jnp.where(i == j, along, 0), axis=1, keepdims=True)
     slot = jnp.sum(jnp.where((down == along) & (i < j), 1, 0), axis=0, keepdims=True)
-    device = lax.broadcasted_iota(jnp.int32, (N_DP, TX), 0)
-    goes = device == jnp.broadcast_to(owner, (N_DP, TX))
+    chip = lax.broadcasted_iota(jnp.int32, (CHIPS, TX), 0)
+    owner = jnp.broadcast_to(owner, (CHIPS, TX))
+    slot = jnp.broadcast_to(slot, (CHIPS, TX))
     return [
-        jnp.where(goes & (jnp.broadcast_to(slot, (N_DP, TX)) == s), 1.0, 0.0).astype(BF16)
+        jnp.where((owner == 2 * chip + core) & (slot == s), 1.0, 0.0).astype(BF16)
+        for core in range(2)
         for s in range(2)
     ]
 
 
+LATER = ("parent", "cot", "co", "up", "down", "link", "pq", "pk", "pv", "po")
+
+
 def encoder_kernel(
-    item_ref, owner_ref, row_ref, parent_ref, cot_ref,
-    cgain, cq, ck, cv, co, hgain, up, down, link, pgain, pq, pk, pv, po,
+    item_ref, owner_ref, row_ref, parent_any, cot_any,
+    cgain, cq, ck, cv, co_any, hgain, up_any, down_any, link_any, pgain, pq_any, pk_any, pv_any, po_any,
     states_ref, parent_sum, down_sum, up_sum, att_sum,
-    n1, q, k, v, probs, mix, s_, n2, u, h, slope, dn2, da, dmix, dqkv, hmean,
+    n1, q, k, v, probs, mix, s_, n2, u, h, slope, dhidden, da, dmix, dqkv, hmean,
     pbased, pn, pq_, pk_, pv_, pprobs, pmix, pda, pdmix, pdqkv, pdn,
     parent_mine, down_mine, up_mine, att_mine,
-    out1, in1, out2, in2, x_send, x_recv,
-    *job_scratch,
+    parent_ref, cot_ref, co, up, down, link, pq, pk, pv, po, load_sem,
+    *comm_scratch,
 ):
+    loads = {}
+    for i, (name, source, target) in enumerate(
+        zip(
+            LATER,
+            (parent_any, cot_any, co_any, up_any, down_any, link_any, pq_any, pk_any, pv_any, po_any),
+            (parent_ref, cot_ref, co, up, down, link, pq, pk, pv, po),
+            strict=True,
+        )
+    ):
+        loads[name] = pltpu.make_async_copy(source, target, load_sem.at[i])
+    for name in ("co", "up", "down", "cot", "po", "parent", "link", "pq", "pk", "pv"):
+        loads[name].start()
     at = place()
     barrier = pltpu.get_barrier_semaphore()
     greeted = greet_all(at, barrier)
@@ -317,6 +369,9 @@
         (parent_sum, down_sum, up_sum, att_sum),
         strict=True,
     )
+    there = Exchange(at, comm_scratch[:6])
+    back = Exchange(at, comm_scratch[6:12])
+    job_scratch = comm_scratch[12:]
     per = len(job_scratch) // 4
     parent_job, down_job, up_job, att_job = [
         Summing(at, *job, job_scratch[i * per : (i + 1) * per]) for i, job in enumerate(jobs)
@@ -331,6 +386,7 @@
     k[...] = dot(n1[...], ck[...]).astype(BF16)
     v[...] = dot(n1[...], cv[...]).astype(BF16)
     attend(q, k, v, probs, mix, GROUPS, GROWS, COLS)
+    loads["co"].wait()
     u[:, :W] = dot(mix[...], co[...])
 
     def norm_stream(rows, i):
@@ -341,49 +397,60 @@
         n2[rows] = (stream * rms_scale(stream) * hgain[...].astype(F32)[None, :]).astype(BF16)
 
     each(GROUPS, GROWS, norm_stream, unroll=2)
+    loads["up"].wait()
     u[...] = dot(n2[...], up[...])
 
     def gelu(rows, i):
         for c in range(0, FF, 256):
             value = u[rows, c : c + 256]
-            square = value * value
-            t = jnp.tanh(math.sqrt(2.0 / math.pi) * value * (1.0 + 0.044715 * square))
-            half = 0.5 * (1.0 + t)
-            h[rows, c : c + 256] = (value * half).astype(BF16)
-            inner = math.sqrt(2.0 / math.pi) * (1.0 + 3 * 0.044715 * square)
-            slope[rows, c : c + 256] = (half + 0.5 * value * (1.0 - t * t) * inner).astype(BF16)
-
-    each(ROWS // 32, 32, gelu)
+            t = jnp.tanh(value * (ROOT + ROOT * 0.044715 * (value * value)))
+            h[rows, c : c + 256] = (value * (0.5 + 0.5 * t)).astype(BF16)
+
+    each(ROWS // 32, 32, gelu, unroll=3)
     average = averaging()
     hidden = (dot(average, h[...]) * (1.0 / COLS)).astype(BF16)
     hmean[...] = hidden
+    loads["down"].wait()
     embedding = (dot(average, s_[...]) * (1.0 / COLS) + dot(hidden, down[...])).astype(BF16)
 
     places = placing(owner_ref)
     ids = jnp.broadcast_to(row_ref[...].astype(F32) + 1.0, (128, TX)).astype(BF16)
-    for slot in range(2):
-        moved = dot(places[slot], embedding)
-        out1[:, 2 * slot, :] = moved[:, :128]
-        out1[:, 2 * slot + 1, :] = moved[:, 128:]
-        out1[:, 4 + slot, :] = dot_nt(places[slot], ids)
-        out1[:, 6 + slot, :] = jnp.zeros((N_DP, 128), F32)
+    for p in range(4):
+        there.put(p, dot(places[p], embedding), dot_nt(places[p], ids))
     pl.semaphore_wait(barrier, greeted)
-    exchange_start(at, out1, in1, x_send.at[0], x_recv.at[0])
-    exchange_wait(at, in1, x_send.at[0], x_recv.at[0])
+    there.start()
+
+    def gelu_slope(rows, i):
+        for c in range(0, FF, 256):
+            value = u[rows, c : c + 256]
+            square = value * value
+            t = jnp.tanh(value * (ROOT + ROOT * 0.044715 * square))
+            inner = value * (ROOT + 3 * ROOT * 0.044715 * square)
+            half = 0.5 + 0.5 * t
+            slope[rows, c : c + 256] = (half + 0.5 * (1.0 - t * t) * inner).astype(BF16)
+
+    each(ROWS // 32, 32, gelu_slope, unroll=3)
+    loads["cot"].wait()
+    loads["po"].wait()
+    scale = 1.0 / math.sqrt(CUST * CTOK * 256)
+    pda[...] = (cot_ref[...].astype(F32) * scale).astype(BF16)
+    pdmix[...] = dot_nt(pda[...], po[...]).astype(BF16)
+    for name in ("parent", "link", "pq", "pk", "pv"):
+        loads[name].wait()
+    there.wait()
 
     members = []
-    customer = lax.broadcasted_iota(jnp.int32, (N_DP, CUST), 1).astype(F32) + 1.0
+    customer = lax.broadcasted_iota(jnp.int32, (CHIPS, CUST), 1).astype(F32) + 1.0
     counts, sums = jnp.zeros((CUST, W), F32), jnp.zeros((CUST, W), F32)
-    for slot in range(2):
-        got = jnp.concatenate([in1[:, 2 * slot, :], in1[:, 2 * slot + 1, :]], axis=1).astype(BF16)
-        member = jnp.where(in1[:, 4 + slot, :][:, :CUST] == customer, 1.0, 0.0).astype(BF16)
-        members.append(member)
-        counts = counts + dot_tn(member, jnp.ones((N_DP, W), BF16))
-        sums = sums + dot_tn(member, got)
+    for source in (there.near, there.far):
+        for got, name in there.rows(source):
+            member = jnp.where(name[:, :CUST] == customer, 1.0, 0.0).astype(BF16)
+            members.append(member)
+            counts = counts + dot_tn(member, jnp.ones((CHIPS, W), BF16))
+            sums = sums + dot_tn(member, got)
     divisor = jnp.maximum(counts, 1.0)
     pooled = (sums / divisor).astype(BF16)
     linked = dot(pooled, link[...])
-    scale = 1.0 / math.sqrt(CUST * CTOK * 256)
     pbased_value = (
         (parent_ref[...].astype(F32).reshape(CUST, CTOK, W) + linked[:, None, :])
         .astype(BF16)
@@ -394,13 +461,11 @@
     def norm_based(rows, i):
         x = pbased[rows].astype(F32)
         pn[rows] = (x * rms_scale(x) * pgain[...].astype(F32)[None, :]).astype(BF16)
-        pda[rows] = (cot_ref[rows].astype(F32) * scale).astype(BF16)
 
     each(PGROUPS, GPROWS, norm_based, unroll=2)
     pq_[...] = dot(pn[...], pq[...]).astype(BF16)
     pk_[...] = dot(pn[...], pk[...]).astype(BF16)
     pv_[...] = dot(pn[...], pv[...]).astype(BF16)
-    pdmix[...] = dot_nt(pda[...], po[...]).astype(BF16)
     attend(pq_, pk_, pv_, pprobs, pmix, PGROUPS, GPROWS, CTOK)
     attend_back(pq_, pk_, pv_, pprobs, pdmix, pdqkv, PGROUPS, GPROWS)
     pdn[...] = (
@@ -422,13 +487,12 @@
     dlinked = jnp.concatenate(dlinked, axis=0)
     dpooled = dot_nt(dlinked.astype(BF16), link[...]).astype(BF16).astype(F32)
     sum_grad = (dpooled / divisor).astype(BF16)
-    for slot in range(2):
-        moved = dot(members[slot], sum_grad)
-        out2[:, 2 * slot, :] = moved[:, :128]
-        out2[:, 2 * slot + 1, :] = moved[:, 128:]
-        out2[:, 4 + slot, :] = jnp.zeros((N_DP, 128), F32)
-        out2[:, 6 + slot, :] = jnp.zeros((N_DP, 128), F32)
-    exchange_start(at, out2, in2, x_send.at[1], x_recv.at[1])
+    core = at[3]
+    moved = [dot(member, sum_grad) for member in members]
+    for p in range(4):
+        home, slot = p // 2, p % 2
+        back.put(p, jnp.where(core == home, moved[slot], moved[2 + slot]))
+    back.start()
 
     put_block(parent_mine, 0, dot_tn(pooled, dlinked.astype(BF16)))
     dweights = dot_tn(pn[...], pdqkv[...])
@@ -438,35 +502,40 @@
     parent_job.start()
     states_ref[...] = (pbased[...].astype(F32) + dot(pmix[...], po[...])).astype(BF16)
     parent_job.scatter_plane()
-    exchange_wait(at, in2, x_send.at[1], x_recv.at[1])
+    back.wait()
 
     ditem = jnp.zeros((TX, W), F32)
-    for slot in range(2):
-        got = jnp.concatenate([in2[:, 2 * slot, :], in2[:, 2 * slot + 1, :]], axis=1).astype(BF16)
-        ditem = ditem + dot_tn(places[slot], got)
+    near, far = back.rows(back.near), back.rows(back.far)
+    for p in range(4):
+        home, slot = p // 2, p % 2
+        got = jnp.where(core == home, near[slot][0].astype(F32), far[slot][0].astype(F32))
+        ditem = ditem + dot_tn(places[p], got.astype(BF16))
     ditem_b = ditem.astype(BF16)
     ddown = dot_tn(hmean[...], ditem_b)
     for b in range(4):
         put_block(down_mine, b, ddown[b * W : (b + 1) * W])
     down_job.start()
-    dhidden = (dot_nt(ditem_b, down[...]) * (1.0 / COLS)).astype(BF16)
-    spread = averaging()
-    u[...] = dot_tn(spread, dhidden)
-    dy = dot_tn(spread, ditem_b)
+    dhidden[...] = (dot_nt(ditem_b, down[...]) * (1.0 / COLS)).astype(BF16).astype(F32)
+    dy = dot_tn(averaging(), ditem_b)
+    parent_job.scatter_z()
 
     def back_hidden(rows, i):
         for c in range(0, FF, 256):
-            h[rows, c : c + 256] = (
-                u[rows, c : c + 256] * slope[rows, c : c + 256].astype(F32)
-            ).astype(BF16)
-
-    each(ROWS // 32, 32, back_hidden)
+            spread = jnp.concatenate(
+                [
+                    jnp.broadcast_to(dhidden[pl.ds(2 * i + t, 1), c : c + 256], (COLS, 256))
+                    for t in range(2)
+                ],
+                axis=0,
+            )
+            h[rows, c : c + 256] = (spread * slope[rows, c : c + 256].astype(F32)).astype(BF16)
+
+    each(TX // 2, 2 * COLS, back_hidden, unroll=3)
     down_job.scatter_plane()
     dup = dot_tn(n2[...], h[...])
     for b in range(4):
         put_block(up_mine, b, dup[:, b * W : (b + 1) * W])
     up_job.start()
-    parent_job.scatter_z()
     u[:, :W] = dot_nt(h[...], up[...])
     u[:, W : 2 * W] = dy
 
@@ -482,14 +551,13 @@
     up_job.scatter_plane()
     dmix[...] = dot_nt(da[...], co[...]).astype(BF16)
     put_block(att_mine, 3, dot_tn(mix[...], da[...]))
-    attend_back(q, k, v, probs, dmix, dqkv, GROUPS, GROWS)
+    meanwhile = {2: down_job.scatter_z, 4: parent_job.gather_plane}
+    attend_back(q, k, v, probs, dmix, dqkv, GROUPS, GROWS, lambda i: meanwhile.get(i, int)())
     dweights = dot_tn(n1[...], dqkv[...])
     for b in range(3):
         put_block(att_mine, b, dweights[:, b * W : (b + 1) * W])
     att_job.start()
 
-    parent_job.gather_plane()
-    down_job.scatter_z()
     att_job.scatter_plane()
     up_job.scatter_z()
     parent_job.gather_core()
@@ -549,6 +617,7 @@
     parent_gain, parent_query, parent_key, parent_value, parent_out,
 ):
     vmem = pl.BlockSpec(memory_space=pltpu.VMEM)
+    later = pl.BlockSpec(memory_space=pl.ANY)
     shape = jax.ShapeDtypeStruct
     cgain, hgain, pgain = column_gain, hidden_gain, parent_gain
     items = lambda width, dtype=BF16: pltpu.VMEM((ROWS, width), dtype)
@@ -557,18 +626,16 @@
         items(W), items(W), items(W), items(W),
         pltpu.VMEM((GROUPS, HEADS * GROWS, GROWS), BF16),
         items(W), items(W), items(W), items(FF, F32), items(FF), items(FF),
-        items(W), items(W), items(W), items(3 * W),
+        pltpu.VMEM((TX, FF), F32), items(W), items(W), items(3 * W),
         pltpu.VMEM((TX, FF), BF16),
         parents(W), parents(W), parents(W), parents(W), parents(W),
         pltpu.VMEM((PGROUPS, HEADS * GPROWS, GPROWS), BF16),
         parents(W), parents(W), parents(W), parents(3 * W), parents(W, F32),
         *[pltpu.VMEM((2, 16, n, 16, 128), BF16) for n in (5, 4, 4, 4)],
-        pltpu.VMEM((N_DP, 8, 128), F32),
-        pltpu.VMEM((N_DP, 8, 128), F32),
-        pltpu.VMEM((N_DP, 8, 128), F32),
-        pltpu.VMEM((N_DP, 8, 128), F32),
-        pltpu.SemaphoreType.DMA((2,)),
-        pltpu.SemaphoreType.DMA((2,)),
+        parents(W), parents(W), pltpu.VMEM((W, W), BF16), pltpu.VMEM((W, FF), BF16),
+        pltpu.VMEM((FF, W), BF16), *[pltpu.VMEM((W, W), BF16) for _ in range(5)],
+        pltpu.SemaphoreType.DMA((len(LATER),)),
+        *Exchange.scratch(), *Exchange.scratch(),
     ]
     for n in (5, 4, 4, 4):
         scratch += Summing.scratch(n)
@@ -576,7 +643,8 @@
         encoder_kernel,
         out_shape=[shape((PROWS, W), BF16)]
         + [shape((2, 16, n, 16, 128), BF16) for n in (5, 4, 4, 4)],
-        in_specs=[vmem] * 19,
+        in_specs=[vmem] * 3 + [later] * 2 + [vmem] * 4 + [later] + [vmem] + [later] * 3 + [vmem]
+        + [later] * 4,
         out_specs=[vmem] * 5,
         scratch_shapes=scratch,
         compiler_params=pltpu.CompilerParams(

time: 86.7 us -> 74.8 us (0.86)
  Pallas kernels: 85.9 us -> 73.9 us
    pallas_call x1, Pallas kernels: 81.4 us -> 69.4 us  [body(): pl.pallas_call(encoder_kernel, out_shape=[shape((PROWS, W), BF16)] + [sha...]
where the time goes in v4:
time: 74.8 us; the launch traced here: 74.7 us
  Pallas kernels  73.9 us (99%)
  between operations  0.8 us (1%)
    pallas_call x1, Pallas kernels, body(): pl.pallas_call(encoder_kernel, out_shape=[shape((PROWS, W), BF16)] + [sha...  69.4 us
    pallas_call x1, Pallas kernels, body(): pl.pallas_call(unpack_kernel, out_shape=[shape((PROWS, W), BF16), row, sq...  4.52 us

profile of v4, /device:TPU:1, one launch (start us, length us, event | category | flops | bytes accessed | tf_op | source)
XLA Modules:
  0.0 74.7 jit_solution(16619347886611791730)
XLA Ops:
  0.6 69.4 %encoder.1 = (bf16[512,256]{1,0:T(8,128)(2,1)}, bf16[2,16,5,16,128]{4,3,2,1,0:T(8,128)(2,1)}, bf16[2,16,4,16,128]{4,3,2,1,0:T(8,128)(2,1)}, bf16[2,16,4,16,128]{...) custom-call(bf16[24,24,256]{2,1,0:T(8,128)(2,1)} %item_ref.1, s32[1,24]{1,0:T(1,128)} %bitcast.10, s32[1,24]{1,0:T(1,128)} %bitcast.11, ...), custom_call_target="tpu_custom_call" | custom-call | tf_op jit(solution)/shard_map/encoder/pallas_call | solution.py:642
  70.0 4.5 %unpack.1 = (bf16[512,256]{1,0:T(8,128)(2,1)}, f32[1,256]{1,0:T(1,128)}, f32[256,256]{1,0:T(8,128)}, f32[256,256]{1,0:T(8,128)}, f32[256,256]{1,0:T(8,128)}, /*i...) custom-call(bf16[512,256]{1,0:T(8,128)(2,1)} %get-tuple-element.35.s, ...), custom_call_target="tpu_custom_call" | custom-call | tf_op jit(solution)/shard_map/unpack/pallas_call | solution.py:663

commit v5 on v4

--- a/solution.py
+++ b/solution.py
@@ -212,6 +212,7 @@
 
 
 VMEM_LIMIT = 56 * 1024 * 1024
+UNPACK_LIMIT = 50 * 1024 * 1024
 EPSILON = 1e-06
 ROOT = math.sqrt(2.0 / math.pi)
 HEADS = 8
@@ -241,12 +242,9 @@
     return lax.dot_general(a, b, (((0,), (0,)), ((), ())), preferred_element_type=F32)
 
 
-def each(count, step, body, unroll=1):
-    def one(i, carry):
-        body(pl.ds(pl.multiple_of(i * step, step), step), i)
-        return carry
-
-    lax.fori_loop(0, count, one, 0, unroll=unroll)
+def each(count, step, body):
+    for i in range(count):
+        body(slice(i * step, (i + 1) * step), i)
 
 
 def head_masks():
@@ -335,36 +333,41 @@
     ]
 
 
-LATER = ("parent", "cot", "co", "up", "down", "link", "pq", "pk", "pv", "po")
+BLOCKS = (5, 4, 5, 3)
+LATER = ("cq", "ck", "cv", "parent", "cot", "co", "up", "down", "link", "pq", "pk", "pv", "po")
 
 
 def encoder_kernel(
     item_ref, owner_ref, row_ref, parent_any, cot_any,
-    cgain, cq, ck, cv, co_any, hgain, up_any, down_any, link_any, pgain, pq_any, pk_any, pv_any, po_any,
-    states_ref, parent_sum, down_sum, up_sum, att_sum,
+    cgain, cq_any, ck_any, cv_any, co_any, hgain, up_any, down_any, link_any, pgain, pq_any, pk_any, pv_any, po_any,
+    states_ref, parent_sum, down_sum, up_sum, att_sum, kept, up, gains,
     n1, q, k, v, probs, mix, s_, n2, u, h, slope, dhidden, da, dmix, dqkv, hmean,
     pbased, pn, pq_, pk_, pv_, pprobs, pmix, pda, pdmix, pdqkv, pdn,
     parent_mine, down_mine, up_mine, att_mine,
-    parent_ref, cot_ref, co, up, down, link, pq, pk, pv, po, load_sem,
+    parent_ref, cot_ref, co, down, link, po, load_sem,
     *comm_scratch,
 ):
+    cq, ck, cv, pq, pk, pv = (kept.at[i] for i in range(6))
     loads = {}
     for i, (name, source, target) in enumerate(
         zip(
             LATER,
-            (parent_any, cot_any, co_any, up_any, down_any, link_any, pq_any, pk_any, pv_any, po_any),
-            (parent_ref, cot_ref, co, up, down, link, pq, pk, pv, po),
+            (
+                cq_any, ck_any, cv_any, parent_any, cot_any, co_any, up_any, down_any, link_any,
+                pq_any, pk_any, pv_any, po_any,
+            ),
+            (cq, ck, cv, parent_ref, cot_ref, co, up, down, link, pq, pk, pv, po),
             strict=True,
         )
     ):
         loads[name] = pltpu.make_async_copy(source, target, load_sem.at[i])
-    for name in ("co", "up", "down", "cot", "po", "parent", "link", "pq", "pk", "pv"):
+    for name in ("cq", "ck", "cv", "co", "up", "down", "cot", "po", "parent", "link", "pq", "pk", "pv"):
         loads[name].start()
     at = place()
     barrier = pltpu.get_barrier_semaphore()
     greeted = greet_all(at, barrier)
     jobs = zip(
-        (5, 4, 4, 4),
+        BLOCKS,
         (parent_mine, down_mine, up_mine, att_mine),
         (parent_sum, down_sum, up_sum, att_sum),
         strict=True,
@@ -378,10 +381,14 @@
     ]
 
     def norm_items(rows, i):
-        x = item_ref[pl.ds(i * GROUP, GROUP)].astype(F32).reshape(GROWS, W)
+        x = item_ref[i * GROUP : (i + 1) * GROUP].astype(F32).reshape(GROWS, W)
         n1[rows] = (x * rms_scale(x) * cgain[...].astype(F32)[None, :]).astype(BF16)
 
-    each(GROUPS, GROWS, norm_items, unroll=2)
+    each(GROUPS, GROWS, norm_items)
+    for i, gain in enumerate((cgain, pgain, hgain)):
+        gains[i : i + 1] = gain[...].astype(F32)[None, :]
+    for name in ("cq", "ck", "cv"):
+        loads[name].wait()
     q[...] = dot(n1[...], cq[...]).astype(BF16)
     k[...] = dot(n1[...], ck[...]).astype(BF16)
     v[...] = dot(n1[...], cv[...]).astype(BF16)
@@ -390,13 +397,13 @@
     u[:, :W] = dot(mix[...], co[...])
 
     def norm_stream(rows, i):
-        x = item_ref[pl.ds(i * GROUP, GROUP)].astype(F32).reshape(GROWS, W)
+        x = item_ref[i * GROUP : (i + 1) * GROUP].astype(F32).reshape(GROWS, W)
         stream = (x + u[rows, :W]).astype(BF16)
         s_[rows] = stream
         stream = stream.astype(F32)
         n2[rows] = (stream * rms_scale(stream) * hgain[...].astype(F32)[None, :]).astype(BF16)
 
-    each(GROUPS, GROWS, norm_stream, unroll=2)
+    each(GROUPS, GROWS, norm_stream)
     loads["up"].wait()
     u[...] = dot(n2[...], up[...])
 
@@ -406,7 +413,7 @@
             t = jnp.tanh(value * (ROOT + ROOT * 0.044715 * (value * value)))
             h[rows, c : c + 256] = (value * (0.5 + 0.5 * t)).astype(BF16)
 
-    each(ROWS // 32, 32, gelu, unroll=3)
+    each(ROWS // 32, 32, gelu)
     average = averaging()
     hidden = (dot(average, h[...]) * (1.0 / COLS)).astype(BF16)
     hmean[...] = hidden
@@ -429,7 +436,7 @@
             half = 0.5 + 0.5 * t
             slope[rows, c : c + 256] = (half + 0.5 * (1.0 - t * t) * inner).astype(BF16)
 
-    each(ROWS // 32, 32, gelu_slope, unroll=3)
+    each(ROWS // 32, 32, gelu_slope)
     loads["cot"].wait()
     loads["po"].wait()
     scale = 1.0 / math.sqrt(CUST * CTOK * 256)
@@ -462,7 +469,7 @@
         x = pbased[rows].astype(F32)
         pn[rows] = (x * rms_scale(x) * pgain[...].astype(F32)[None, :]).astype(BF16)
 
-    each(PGROUPS, GPROWS, norm_based, unroll=2)
+    each(PGROUPS, GPROWS, norm_based)
     pq_[...] = dot(pn[...], pq[...]).astype(BF16)
     pk_[...] = dot(pn[...], pk[...]).astype(BF16)
     pv_[...] = dot(pn[...], pv[...]).astype(BF16)
@@ -517,25 +524,18 @@
     down_job.start()
     dhidden[...] = (dot_nt(ditem_b, down[...]) * (1.0 / COLS)).astype(BF16).astype(F32)
     dy = dot_tn(averaging(), ditem_b)
-    parent_job.scatter_z()
 
     def back_hidden(rows, i):
-        for c in range(0, FF, 256):
-            spread = jnp.concatenate(
-                [
-                    jnp.broadcast_to(dhidden[pl.ds(2 * i + t, 1), c : c + 256], (COLS, 256))
-                    for t in range(2)
-                ],
-                axis=0,
-            )
-            h[rows, c : c + 256] = (spread * slope[rows, c : c + 256].astype(F32)).astype(BF16)
-
-    each(TX // 2, 2 * COLS, back_hidden, unroll=3)
+        spread = jnp.concatenate(
+            [jnp.broadcast_to(dhidden[t : t + 1], (COLS, FF)) for t in (2 * i, 2 * i + 1)], axis=0
+        )
+        h[rows] = (spread * slope[rows].astype(F32)).astype(BF16)
+
+    each(TX // 2, 2 * COLS, back_hidden)
     down_job.scatter_plane()
     dup = dot_tn(n2[...], h[...])
     for b in range(4):
         put_block(up_mine, b, dup[:, b * W : (b + 1) * W])
-    up_job.start()
     u[:, :W] = dot_nt(h[...], up[...])
     u[:, W : 2 * W] = dy
 
@@ -547,11 +547,12 @@
         dx = r * (dunit - unit * jnp.mean(dunit * unit, axis=1, keepdims=True))
         da[rows] = (dx + u[rows, W : 2 * W] * (1.0 / COLS)).astype(BF16)
 
-    each(GROUPS, GROWS, back_stream, unroll=2)
+    each(GROUPS, GROWS, back_stream)
+    put_block(up_mine, 4, dot_tn(mix[...], da[...]))
+    up_job.start()
+    dmix[...] = dot_nt(da[...], co[...]).astype(BF16)
     up_job.scatter_plane()
-    dmix[...] = dot_nt(da[...], co[...]).astype(BF16)
-    put_block(att_mine, 3, dot_tn(mix[...], da[...]))
-    meanwhile = {2: down_job.scatter_z, 4: parent_job.gather_plane}
+    meanwhile = {1: parent_job.scatter_z, 4: down_job.scatter_z}
     attend_back(q, k, v, probs, dmix, dqkv, GROUPS, GROWS, lambda i: meanwhile.get(i, int)())
     dweights = dot_tn(n1[...], dqkv[...])
     for b in range(3):
@@ -559,10 +560,11 @@
     att_job.start()
 
     att_job.scatter_plane()
+    parent_job.gather_plane()
     up_job.scatter_z()
-    parent_job.gather_core()
     down_job.gather_plane()
     att_job.scatter_z()
+    parent_job.gather_core()
     up_job.gather_plane()
     down_job.gather_core()
     att_job.gather_plane()
@@ -579,35 +581,49 @@
     high = total.astype(BF16)
     low = (total - high.astype(F32)).astype(BF16)
     ones = jnp.ones((8, W), BF16)
-    return (dot_nt(ones, high) + dot_nt(ones, low))[:1] / gain.astype(F32)[None, :]
+    return (dot_nt(ones, high) + dot_nt(ones, low))[:1] / gain
 
 
 def unpack_kernel(
-    states_in, parent_sum, down_sum, up_sum, att_sum, cgain, cq, ck, cv, hgain, up, pgain, pq, pk, pv,
+    states_in, parent_sum, down_sum, up_sum, att_sum, kept, up, gains,
     states, dcg, dcq, dck, dcv, dco, dhg, dup, ddown, dlink, dpg, dpq, dpk, dpv, dpo,
+    stage, wide_stage, tall_stage, gain_stage, store_sem,
 ):
     def block(total, b):
         return jnp.concatenate(
             [total[half, :, b].astype(F32).reshape(W, 128) for half in range(2)], axis=1
         )
 
-    states[...] = states_in[...]
-    grads = []
-    for b, ref in enumerate((dcq, dck, dcv, dco)):
-        grads.append(block(att_sum, b))
-        ref[...] = grads[-1]
-    dcg[...] = gain_row([cq[...], ck[...], cv[...]], grads[:3], cgain[...])
-    grads = []
+    copies = []
+
+    def store(source, target):
+        copies.append(pltpu.make_async_copy(source, target, store_sem.at[len(copies)]))
+        copies[-1].start()
+
+    store(states_in, states)
     for b in range(4):
-        ddown[b * W : (b + 1) * W] = block(down_sum, b)
-        grads.append(block(up_sum, b))
-        dup[:, b * W : (b + 1) * W] = grads[-1]
-    dhg[...] = gain_row([up[:, b * W : (b + 1) * W] for b in range(4)], grads, hgain[...])
-    grads = []
-    for b, ref in enumerate((dlink, dpq, dpk, dpv, dpo)):
-        grads.append(block(parent_sum, b))
-        ref[...] = grads[-1]
-    dpg[...] = gain_row([pq[...], pk[...], pv[...]], grads[1:4], pgain[...])
+        tall_stage[b * W : (b + 1) * W] = block(down_sum, b)
+    store(tall_stage, ddown)
+    for b in range(4):
+        wide_stage[:, b * W : (b + 1) * W] = block(up_sum, b)
+    store(wide_stage, dup)
+    squares = [(att_sum, b, ref) for b, ref in enumerate((dcq, dck, dcv))]
+    squares += [(parent_sum, b, ref) for b, ref in enumerate((dlink, dpq, dpk, dpv, dpo))]
+    squares += [(up_sum, 4, dco)]
+    for i, (total, b, ref) in enumerate(squares):
+        stage[i] = block(total, b)
+        store(stage.at[i], ref)
+    for i in range(2):
+        grads = [stage[j] for j in ((0, 1, 2), (4, 5, 6))[i]]
+        gain_stage[i] = gain_row([kept[3 * i + j] for j in range(3)], grads, gains[i : i + 1])
+    cuts = [slice(b * W, (b + 1) * W) for b in range(4)]
+    gain_stage[2] = gain_row(
+        [up[:, c] for c in cuts], [wide_stage[:, c] for c in cuts], gains[2:3]
+    )
+    for i, ref in enumerate((dcg, dpg, dhg)):
+        store(gain_stage.at[i], ref)
+    for done in copies:
+        done.wait()
 
 
 def body(
@@ -631,21 +647,22 @@
         parents(W), parents(W), parents(W), parents(W), parents(W),
         pltpu.VMEM((PGROUPS, HEADS * GPROWS, GPROWS), BF16),
         parents(W), parents(W), parents(W), parents(3 * W), parents(W, F32),
-        *[pltpu.VMEM((2, 16, n, 16, 128), BF16) for n in (5, 4, 4, 4)],
-        parents(W), parents(W), pltpu.VMEM((W, W), BF16), pltpu.VMEM((W, FF), BF16),
-        pltpu.VMEM((FF, W), BF16), *[pltpu.VMEM((W, W), BF16) for _ in range(5)],
+        *[pltpu.VMEM((2, 16, n, 16, 128), BF16) for n in BLOCKS],
+        parents(W), parents(W), pltpu.VMEM((W, W), BF16), pltpu.VMEM((FF, W), BF16),
+        pltpu.VMEM((W, W), BF16), pltpu.VMEM((W, W), BF16),
         pltpu.SemaphoreType.DMA((len(LATER),)),
         *Exchange.scratch(), *Exchange.scratch(),
     ]
-    for n in (5, 4, 4, 4):
+    for n in BLOCKS:
         scratch += Summing.scratch(n)
-    states, parent_sum, down_sum, up_sum, att_sum = pl.pallas_call(
+    kept = pl.pallas_call(
         encoder_kernel,
-        out_shape=[shape((PROWS, W), BF16)]
-        + [shape((2, 16, n, 16, 128), BF16) for n in (5, 4, 4, 4)],
-        in_specs=[vmem] * 3 + [later] * 2 + [vmem] * 4 + [later] + [vmem] + [later] * 3 + [vmem]
+        out_shape=[pltpu.VMEM((PROWS, W), BF16)]
+        + [pltpu.VMEM((2, 16, n, 16, 128), BF16) for n in BLOCKS]
+        + [pltpu.VMEM((6, W, W), BF16), pltpu.VMEM((W, FF), BF16), pltpu.VMEM((3, W), F32)],
+        in_specs=[vmem] * 3 + [later] * 2 + [vmem] + [later] * 4 + [vmem] + [later] * 3 + [vmem]
         + [later] * 4,
-        out_specs=[vmem] * 5,
+        out_specs=[vmem] * 8,
         scratch_shapes=scratch,
         compiler_params=pltpu.CompilerParams(
             collective_id=1, has_side_effects=True, vmem_limit_bytes=VMEM_LIMIT
@@ -666,14 +683,15 @@
             shape((PROWS, W), BF16), row, square, square, square, square, row,
             shape((W, FF), F32), shape((FF, W), F32), square, row, square, square, square, square,
         ],
-        in_specs=[vmem] * 15,
-        out_specs=[vmem] * 15,
-        compiler_params=pltpu.CompilerParams(vmem_limit_bytes=VMEM_LIMIT),
+        in_specs=[vmem] * 8,
+        out_specs=[later] * 15,
+        scratch_shapes=[
+            pltpu.VMEM((9, W, W), F32), pltpu.VMEM((W, FF), F32), pltpu.VMEM((FF, W), F32),
+            pltpu.VMEM((3, 1, W), F32), pltpu.SemaphoreType.DMA((15,)),
+        ],
+        compiler_params=pltpu.CompilerParams(vmem_limit_bytes=UNPACK_LIMIT),
         name="unpack",
-    )(
-        states, parent_sum, down_sum, up_sum, att_sum, cgain, column_query, column_key, column_value,
-        hgain, up_weight, pgain, parent_query, parent_key, parent_value,
-    )
+    )(*kept)
     out = [o.reshape(W) if o.shape == (1, W) else o for o in out]
     return (out[0].reshape(CUST, CTOK, W), *out[1:])
 

time: 74.8 us -> 70.3 us (0.940)
  Pallas kernels: 73.9 us -> 69.3 us
    pallas_call x1, Pallas kernels: 69.4 us -> 67 us  [body(): pl.pallas_call(encoder_kernel, out_shape=[pltpu.VMEM((PROWS, W), BF16)] +...]
    pallas_call x1, Pallas kernels: 4.52 us -> 2.31 us  [body(): pl.pallas_call(unpack_kernel, out_shape=[shape((PROWS, W), BF16), row, sq...]
where the time goes in v5:
time: 70.3 us; the launch traced here: 70.1 us
  Pallas kernels  69.3 us (99%)
  between operations  0.82 us (1%)
    pallas_call x1, Pallas kernels, body(): pl.pallas_call(encoder_kernel, out_shape=[pltpu.VMEM((PROWS, W), BF16)] +...  67 us
    pallas_call x1, Pallas kernels, body(): pl.pallas_call(unpack_kernel, out_shape=[shape((PROWS, W), BF16), row, sq...  2.31 us

profile of v5, /device:TPU:1, one launch (start us, length us, event | category | flops | bytes accessed | tf_op | source)
XLA Modules:
  0.0 70.1 jit_solution(5543118721929117332)
XLA Ops:
  0.7 67.0 %encoder.1 = (bf16[512,256]{1,0:T(8,128)(2,1)S(1)}, bf16[2,16,5,16,128]{4,3,2,1,0:T(8,128)(2,1)S(1)}, bf16[2,16,4,16,128]{4,3,2,1,0:T(8,128)(2,1)S(1)}, bf16[2,1...) custom-call(bf16[24,24,256]{2,1,0:T(8,128)(2,1)} %item_ref.1, ...), custom_call_target="tpu_custom_call" | custom-call | tf_op jit(solution)/shard_map/encoder/pallas_call | solution.py:658
  67.7 2.3 %unpack.1 = (bf16[512,256]{1,0:T(8,128)(2,1)}, f32[1,256]{1,0:T(1,128)}, f32[256,256]{1,0:T(8,128)}, f32[256,256]{1,0:T(8,128)}, f32[256,256]{1,0:T(8,128)}, /*i...) custom-call(bf16[512,256]{1,0:T(8,128)(2,1)S(1)} %get-tuple-element., ...), custom_call_target="tpu_custom_call" | custom-call | tf_op jit(solution)/shard_map/unpack/pallas_call | solution.py:680

commit v6 on v5

--- a/solution.py
+++ b/solution.py
@@ -179,12 +179,16 @@
     def wait(self):
         rest = self.near.at[pl.ds(0, CHIPS - 1)]
         wait_received(self.at, rest, self.recv.at[0])
-        across = remote(
+        self.across = remote(
             self.near, self.far, self.send.at[1], self.recv.at[1], core_peer(self.at)
         )
-        wait_sent(self.at, rest, self.send.at[0])
-        across.wait_recv()
-        across.wait_send()
+
+    def wait_far(self):
+        self.across.wait_recv()
+
+    def finish(self):
+        wait_sent(self.at, self.near.at[pl.ds(0, CHIPS - 1)], self.send.at[0])
+        self.across.wait_send()
 
     def rows(self, source):
         dp, rep, z, core, spot = self.at
@@ -450,6 +454,8 @@
     customer = lax.broadcasted_iota(jnp.int32, (CHIPS, CUST), 1).astype(F32) + 1.0
     counts, sums = jnp.zeros((CUST, W), F32), jnp.zeros((CUST, W), F32)
     for source in (there.near, there.far):
+        if source is there.far:
+            there.wait_far()
         for got, name in there.rows(source):
             member = jnp.where(name[:, :CUST] == customer, 1.0, 0.0).astype(BF16)
             members.append(member)
@@ -512,7 +518,9 @@
     back.wait()
 
     ditem = jnp.zeros((TX, W), F32)
-    near, far = back.rows(back.near), back.rows(back.far)
+    near = back.rows(back.near)
+    back.wait_far()
+    far = back.rows(back.far)
     for p in range(4):
         home, slot = p // 2, p % 2
         got = jnp.where(core == home, near[slot][0].astype(F32), far[slot][0].astype(F32))
@@ -532,12 +540,13 @@
         h[rows] = (spread * slope[rows].astype(F32)).astype(BF16)
 
     each(TX // 2, 2 * COLS, back_hidden)
-    down_job.scatter_plane()
     dup = dot_tn(n2[...], h[...])
     for b in range(4):
         put_block(up_mine, b, dup[:, b * W : (b + 1) * W])
     u[:, :W] = dot_nt(h[...], up[...])
     u[:, W : 2 * W] = dy
+    parent_job.scatter_z()
+    down_job.scatter_plane()
 
     def back_stream(rows, i):
         x = s_[rows].astype(F32)
@@ -551,8 +560,7 @@
     put_block(up_mine, 4, dot_tn(mix[...], da[...]))
     up_job.start()
     dmix[...] = dot_nt(da[...], co[...]).astype(BF16)
-    up_job.scatter_plane()
-    meanwhile = {1: parent_job.scatter_z, 4: down_job.scatter_z}
+    meanwhile = {1: up_job.scatter_plane, 5: down_job.scatter_z}
     attend_back(q, k, v, probs, dmix, dqkv, GROUPS, GROWS, lambda i: meanwhile.get(i, int)())
     dweights = dot_tn(n1[...], dqkv[...])
     for b in range(3):
@@ -562,15 +570,15 @@
     att_job.scatter_plane()
     parent_job.gather_plane()
     up_job.scatter_z()
+    att_job.scatter_z()
     down_job.gather_plane()
-    att_job.scatter_z()
+    up_job.gather_plane()
     parent_job.gather_core()
-    up_job.gather_plane()
     down_job.gather_core()
     att_job.gather_plane()
     up_job.gather_core()
     att_job.gather_core()
-    for job in (parent_job, down_job, up_job, att_job):
+    for job in (there, back, parent_job, down_job, up_job, att_job):
         job.finish()
 
 

time: 70.3 us -> 66.8 us (0.950)
  Pallas kernels: 69.3 us -> 65.8 us
    pallas_call x1, Pallas kernels: 67 us -> 63.5 us  [body(): pl.pallas_call(encoder_kernel, out_shape=[pltpu.VMEM((PROWS, W), BF16)] +...]
where the time goes in v6:
time: 66.8 us; the launch traced here: 66.7 us
  Pallas kernels  65.8 us (99%)
  between operations  0.82 us (1%)
    pallas_call x1, Pallas kernels, body(): pl.pallas_call(encoder_kernel, out_shape=[pltpu.VMEM((PROWS, W), BF16)] +...  63.5 us
    pallas_call x1, Pallas kernels, body(): pl.pallas_call(unpack_kernel, out_shape=[shape((PROWS, W), BF16), row, sq...  2.31 us

profile of v6, /device:TPU:1, one launch (start us, length us, event | category | flops | bytes accessed | tf_op | source)
XLA Modules:
  0.0 66.7 jit_solution(687868244599767594)
XLA Ops:
  0.7 63.5 %encoder.1 = (bf16[512,256]{1,0:T(8,128)(2,1)S(1)}, bf16[2,16,5,16,128]{4,3,2,1,0:T(8,128)(2,1)S(1)}, bf16[2,16,4,16,128]{4,3,2,1,0:T(8,128)(2,1)S(1)}, bf16[2,1...) custom-call(bf16[24,24,256]{2,1,0:T(8,128)(2,1)} %item_ref.1, ...), custom_call_target="tpu_custom_call" | custom-call | tf_op jit(solution)/shard_map/encoder/pallas_call | solution.py:666
  64.2 2.3 %unpack.1 = (bf16[512,256]{1,0:T(8,128)(2,1)}, f32[1,256]{1,0:T(1,128)}, f32[256,256]{1,0:T(8,128)}, f32[256,256]{1,0:T(8,128)}, f32[256,256]{1,0:T(8,128)}, /*i...) custom-call(bf16[512,256]{1,0:T(8,128)(2,1)S(1)} %get-tuple-element., ...), custom_call_target="tpu_custom_call" | custom-call | tf_op jit(solution)/shard_map/unpack/pallas_call | solution.py:688

commit v7 on v6

--- a/solution.py
+++ b/solution.py
@@ -338,17 +338,17 @@
 
 
 BLOCKS = (5, 4, 5, 3)
-LATER = ("cq", "ck", "cv", "parent", "cot", "co", "up", "down", "link", "pq", "pk", "pv", "po")
+LATER = ("item", "cq", "ck", "cv", "parent", "cot", "co", "up", "down", "link", "pq", "pk", "pv", "po")
 
 
 def encoder_kernel(
-    item_ref, owner_ref, row_ref, parent_any, cot_any,
+    item_any, owner_ref, row_ref, parent_any, cot_any,
     cgain, cq_any, ck_any, cv_any, co_any, hgain, up_any, down_any, link_any, pgain, pq_any, pk_any, pv_any, po_any,
     states_ref, parent_sum, down_sum, up_sum, att_sum, kept, up, gains,
     n1, q, k, v, probs, mix, s_, n2, u, h, slope, dhidden, da, dmix, dqkv, hmean,
     pbased, pn, pq_, pk_, pv_, pprobs, pmix, pda, pdmix, pdqkv, pdn,
     parent_mine, down_mine, up_mine, att_mine,
-    parent_ref, cot_ref, co, down, link, po, load_sem,
+    item_ref, parent_ref, cot_ref, co, down, link, po, load_sem,
     *comm_scratch,
 ):
     cq, ck, cv, pq, pk, pv = (kept.at[i] for i in range(6))
@@ -357,15 +357,15 @@
         zip(
             LATER,
             (
-                cq_any, ck_any, cv_any, parent_any, cot_any, co_any, up_any, down_any, link_any,
+                item_any, cq_any, ck_any, cv_any, parent_any, cot_any, co_any, up_any, down_any, link_any,
                 pq_any, pk_any, pv_any, po_any,
             ),
-            (cq, ck, cv, parent_ref, cot_ref, co, up, down, link, pq, pk, pv, po),
+            (item_ref, cq, ck, cv, parent_ref, cot_ref, co, up, down, link, pq, pk, pv, po),
             strict=True,
         )
     ):
         loads[name] = pltpu.make_async_copy(source, target, load_sem.at[i])
-    for name in ("cq", "ck", "cv", "co", "up", "down", "cot", "po", "parent", "link", "pq", "pk", "pv"):
+    for name in ("item", "cq", "ck", "cv", "co", "up", "down", "cot", "po", "parent", "link", "pq", "pk", "pv"):
         loads[name].start()
     at = place()
     barrier = pltpu.get_barrier_semaphore()
@@ -383,6 +383,8 @@
     parent_job, down_job, up_job, att_job = [
         Summing(at, *job, job_scratch[i * per : (i + 1) * per]) for i, job in enumerate(jobs)
     ]
+
+    loads["item"].wait()
 
     def norm_items(rows, i):
         x = item_ref[i * GROUP : (i + 1) * GROUP].astype(F32).reshape(GROWS, W)
@@ -656,6 +658,7 @@
         pltpu.VMEM((PGROUPS, HEADS * GPROWS, GPROWS), BF16),
         parents(W), parents(W), parents(W), parents(3 * W), parents(W, F32),
         *[pltpu.VMEM((2, 16, n, 16, 128), BF16) for n in BLOCKS],
+        pltpu.VMEM((TX, COLS, W), BF16),
         parents(W), parents(W), pltpu.VMEM((W, W), BF16), pltpu.VMEM((FF, W), BF16),
         pltpu.VMEM((W, W), BF16), pltpu.VMEM((W, W), BF16),
         pltpu.SemaphoreType.DMA((len(LATER),)),
@@ -668,7 +671,7 @@
         out_shape=[pltpu.VMEM((PROWS, W), BF16)]
         + [pltpu.VMEM((2, 16, n, 16, 128), BF16) for n in BLOCKS]
         + [pltpu.VMEM((6, W, W), BF16), pltpu.VMEM((W, FF), BF16), pltpu.VMEM((3, W), F32)],
-        in_specs=[vmem] * 3 + [later] * 2 + [vmem] + [later] * 4 + [vmem] + [later] * 3 + [vmem]
+        in_specs=[later] + [vmem] * 2 + [later] * 2 + [vmem] + [later] * 4 + [vmem] + [later] * 3 + [vmem]
         + [later] * 4,
         out_specs=[vmem] * 8,
         scratch_shapes=scratch,

time: 66.8 us -> 67.5 us (1.010)
  Pallas kernels: 65.8 us -> 66.5 us
    pallas_call x1, Pallas kernels: 63.5 us -> 64.2 us  [body(): pl.pallas_call(encoder_kernel, out_shape=[pltpu.VMEM((PROWS, W), BF16)] +...]
where the time goes in v7:
time: 67.5 us; the launch traced here: 67.4 us
  Pallas kernels  66.5 us (99%)
  between operations  0.82 us (1%)
    pallas_call x1, Pallas kernels, body(): pl.pallas_call(encoder_kernel, out_shape=[pltpu.VMEM((PROWS, W), BF16)] +...  64.2 us
    pallas_call x1, Pallas kernels, body(): pl.pallas_call(unpack_kernel, out_shape=[shape((PROWS, W), BF16), row, sq...  2.31 us

profile of v7, /device:TPU:1, one launch (start us, length us, event | category | flops | bytes accessed | tf_op | source)
XLA Modules:
  0.0 67.4 jit_solution(12785095542510048762)
XLA Ops:
  0.7 64.2 %encoder.1 = (bf16[512,256]{1,0:T(8,128)(2,1)S(1)}, bf16[2,16,5,16,128]{4,3,2,1,0:T(8,128)(2,1)S(1)}, bf16[2,16,4,16,128]{4,3,2,1,0:T(8,128)(2,1)S(1)}, bf16[2,1...) custom-call(bf16[24,24,256]{2,1,0:T(8,128)(2,1)} %item_any.1, ...), custom_call_target="tpu_custom_call" | custom-call | tf_op jit(solution)/shard_map/encoder/pallas_call | solution.py:669
  64.9 2.3 %unpack.1 = (bf16[512,256]{1,0:T(8,128)(2,1)}, f32[1,256]{1,0:T(1,128)}, f32[256,256]{1,0:T(8,128)}, f32[256,256]{1,0:T(8,128)}, f32[256,256]{1,0:T(8,128)}, /*i...) custom-call(bf16[512,256]{1,0:T(8,128)(2,1)S(1)} %get-tuple-element., ...), custom_call_target="tpu_custom_call" | custom-call | tf_op jit(solution)/shard_map/unpack/pallas_call | solution.py:691
